TPU v7x, 256 devices: a whole 4x4x8 slice. The times are simulated.
256 devices in a mesh: samp: 2 (over y_lo), row: 8 (over y_hi, x), col: 16 (over z, core).
Axes of the slice: x: 4, y: 4 (y_hi: 2, y_lo: 2; y = y_hi * 2 + y_lo), z: 8, core: 2. Of those that a mesh axis runs over, the one named last changes fastest.
Arguments:
- tokens: bfloat16 [8, 1024, 768], P('samp', 'col'), may hold values from -110 to 110
- restype: int32 [1024], P('col'), may hold values from 0 to 31
- type_table: bfloat16 [32, 768], replicated, may hold values from -8 to 8
- key_mask: int32 [1024], P('col'), may hold values 0 or 1
- pair: bfloat16 [1024, 1024, 128], P('row', 'col'), may hold values from -160 to 160
- w_bias: bfloat16 [128, 16], replicated, may hold values from -0.5 to 0.5
- w_query: bfloat16 [768, 768], replicated, may hold values from -2 to 2
- w_key: bfloat16 [768, 768], replicated, may hold values from -2 to 2
- w_value: bfloat16 [768, 768], replicated, may hold values from -0.21875 to 0.21875
- w_gate: bfloat16 [768, 768], replicated, may hold values from -0.21875 to 0.21875
- cotangent: bfloat16 [8, 1024, 768], P('samp', 'col'), may hold values from -6 to 6
Outputs:
- token_grad: bfloat16 [8, 1024, 768], P('samp', 'col')
- pair_grad: bfloat16 [1024, 1024, 128], P('row', 'col')
- bias_weight_grad: float32 [128, 16], replicated
All inputs are finite; a program needn't handle non-finite values. No bound on the sum of `key_mask` on one device may be relied on, other than what follows from the above.
Results may differ from a plain program's by a relative error of at most 0.034.
The roundings to bfloat16 on the way count: a program that leaves them out, or rounds other values in their place, can miss the bound.
Values may be sent and summed in bfloat16 or wider, within the bound.
A program may use at most 128 MiB of HBM per device.

v0:
```python
import math

import jax
import jax.numpy as jnp
from jax import lax
from jax.sharding import PartitionSpec as P

D = 768
H = 16
CH = 48
NTYPE = 32


def broadcast(block, axis, source):
    block = jnp.where(lax.axis_index(axis) == source, block, jnp.zeros_like(block))
    return lax.psum(block, axis)


def token_norm(tokens, restype, type_table):
    onehot = (restype[:, None] == jnp.arange(NTYPE, dtype=jnp.int32)[None, :]).astype(jnp.bfloat16)
    embedded = tokens.astype(jnp.float32) + jnp.dot(
        onehot, type_table, preferred_element_type=jnp.float32
    )
    centred = embedded - jnp.mean(embedded, axis=-1, keepdims=True)
    inv_std = lax.rsqrt(jnp.mean(centred * centred, axis=-1, keepdims=True) + 1e-05)
    return (centred * inv_std, inv_std)


def pair_norm(block):
    values = block.astype(jnp.float32)
    centred = values - jnp.mean(values, axis=-1, keepdims=True)
    inv_std = lax.rsqrt(jnp.mean(centred * centred, axis=-1, keepdims=True) + 1e-05)
    return (centred * inv_std, inv_std)


def norm_back(grad_in, normed, inv_std):
    return inv_std * (
        grad_in
        - jnp.mean(grad_in, axis=-1, keepdims=True)
        - normed * jnp.mean(grad_in * normed, axis=-1, keepdims=True)
    )


def project(rows_in, weight):
    return jnp.einsum("std,de->ste", rows_in, weight, preferred_element_type=jnp.float32).astype(
        jnp.bfloat16
    )


def back_project(grads, weight):
    return jnp.einsum(
        "ste,de->std", grads, weight.astype(jnp.float32), precision=lax.Precision.HIGHEST
    )


def pair_back(grad_bias, pair_normed, pair_inv, bias_weight):
    grad_normed = jnp.einsum("hij,ch->ijc", grad_bias, bias_weight, precision=lax.Precision.HIGHEST)
    return norm_back(grad_normed, pair_normed, pair_inv)


def body(
    tokens, restype, type_table, key_mask, pair, w_bias, w_query, w_key, w_value, w_gate, cotangent
):
    n_row = lax.axis_size("row")
    n_col = lax.axis_size("col")
    n_samp = lax.axis_size("samp")
    samp_dev = tokens.shape[0]
    tok_col = tokens.shape[1]
    spread = n_col // n_row
    row_count = tok_col * spread
    total_tokens = tok_col * n_col
    row_index = lax.axis_index("row")
    col_index = lax.axis_index("col")
    is_owner = col_index // spread == row_index
    own_start = col_index % spread * tok_col
    normed, inv_std = token_norm(tokens, restype, type_table)
    own_act = normed.astype(jnp.bfloat16)
    key_proj = project(own_act, w_key)
    value_proj = project(own_act, w_value)
    stacked = jnp.stack([own_act, cotangent])
    pieces = [broadcast(stacked, "col", row_index * spread + member) for member in range(spread)]
    gathered = jnp.concatenate(pieces, axis=2)
    query_side = gathered[0]
    grad_rows = gathered[1]
    queries = project(query_side, w_query)
    gate_lin = project(query_side, w_gate)
    pair_normed, pair_inv = pair_norm(pair)
    bias_weight = w_bias.astype(jnp.float32)
    bias = jnp.einsum("ijc,ch->hij", pair_normed, bias_weight, precision=lax.Precision.HIGHEST)
    query_heads = queries.reshape(samp_dev, row_count, H, CH)
    key_heads = key_proj.reshape(samp_dev, tok_col, H, CH)
    value_heads = value_proj.reshape(samp_dev, tok_col, H, CH)
    scores = (
        jnp.einsum("sihc,sjhc->shij", query_heads, key_heads, preferred_element_type=jnp.float32)
        / math.sqrt(CH)
        + bias[None]
    )
    scores = jnp.where(key_mask[None, None, None, :] == 1, scores, -1000000000.0)
    top = lax.pmax(jnp.max(scores, axis=-1), "col")
    expo = jnp.exp(scores - top[..., None])
    partial_out = jnp.einsum(
        "shij,sjhc->sihc",
        expo.astype(jnp.bfloat16),
        value_heads,
        preferred_element_type=jnp.float32,
    )
    totals, summed = lax.psum(
        (jnp.sum(expo, axis=-1), partial_out.reshape(samp_dev, row_count, D)), "col"
    )
    attended = (
        summed.reshape(samp_dev, row_count, H, CH) / jnp.transpose(totals, (0, 2, 1))[..., None]
    )
    flat_out = attended.reshape(samp_dev, row_count, D)
    sig_gate = jax.nn.sigmoid(gate_lin.astype(jnp.float32))
    grad_f = grad_rows.astype(jnp.float32)
    grad_out = (grad_f * sig_gate).astype(jnp.bfloat16)
    grad_gate = (grad_f * flat_out * sig_gate * (1.0 - sig_gate)).astype(jnp.bfloat16)
    gate_piece = lax.dynamic_slice_in_dim(grad_gate, own_start, tok_col, 1)
    gate_term = jnp.where(
        is_owner,
        jnp.einsum("ste,de->std", gate_piece, w_gate, preferred_element_type=jnp.float32),
        0.0,
    )
    grad_heads = grad_out.reshape(samp_dev, row_count, H, CH)
    delta = jnp.transpose(jnp.sum(grad_heads.astype(jnp.float32) * attended, axis=-1), (0, 2, 1))
    probs = expo / totals[..., None]
    grad_pre = jnp.einsum(
        "sihc,sjhc->shij", grad_heads, value_heads, preferred_element_type=jnp.float32
    )
    grad_scores = probs * (grad_pre - delta[..., None])
    rounded = grad_scores.astype(jnp.bfloat16)
    grad_query = (
        jnp.einsum("shij,sjhc->sihc", rounded, key_heads, preferred_element_type=jnp.float32)
        / math.sqrt(CH)
    ).reshape(samp_dev, row_count, D)
    grad_key = (
        jnp.einsum("shij,sihc->sjhc", rounded, query_heads, preferred_element_type=jnp.float32)
        / math.sqrt(CH)
    ).reshape(samp_dev, tok_col, D)
    grad_value = jnp.einsum(
        "shij,sihc->sjhc",
        probs.astype(jnp.bfloat16),
        grad_heads,
        preferred_element_type=jnp.float32,
    ).reshape(samp_dev, tok_col, D)
    bias_local = jnp.sum(grad_scores, axis=0)
    blank = jnp.zeros((samp_dev, total_tokens, D), jnp.float32)
    mine = lax.psum_scatter(
        lax.dynamic_update_slice_in_dim(blank, grad_query, row_index * row_count, 1),
        "col",
        scatter_dimension=1,
        tiled=True,
    )
    query_all, key_all, value_all, gate_all = lax.psum(
        (mine, grad_key, grad_value, gate_term), "row"
    )
    grad_act = (
        back_project(query_all, w_query)
        + back_project(key_all, w_key)
        + back_project(value_all, w_value)
        + gate_all
    )
    token_grad = norm_back(grad_act, normed, inv_std).astype(jnp.bfloat16)
    samples = samp_dev * n_samp
    grad_bias = lax.psum(bias_local, "samp")
    grad_pair = pair_back(grad_bias, pair_normed, pair_inv, bias_weight)
    pair_grad = (grad_pair * (total_tokens / samples)).astype(jnp.bfloat16)
    weight_part = jnp.einsum("ijc,hij->ch", pair_normed, grad_bias, precision=lax.Precision.HIGHEST)
    weight_sum = lax.psum(weight_part, ("row", "col"))
    bias_weight_grad = weight_sum / samples
    return (token_grad, pair_grad, bias_weight_grad)


def solution(mesh):
    placed = (
        P("samp", "col", None),
        P("col"),
        P(),
        P("col"),
        P("row", "col", None),
        P(),
        P(),
        P(),
        P(),
        P(),
        P("samp", "col", None),
    )
    return jax.shard_map(
        body,
        mesh=mesh,
        in_specs=placed,
        out_specs=(P("samp", "col", None), P("row", "col", None), P()),
        check_vma=False,
    )
```

profile of v0, /device:TPU:8, one launch (start us, length us, event | category | flops | bytes accessed | tf_op | source)
XLA Modules:
  0.0 817.9 jit_solution(11296488903200109032)
XLA Ops:
  9.6 1.2 multiply_reduce_fusion.2
  12.0 1.3 broadcast_select_fusion
  13.4 2.6 convolution_convert_fusion.2
  16.0 1.3 convolution_convert_fusion.3
  17.3 3.3 copy.51
  21.1 1.4 fusion.13
  22.5 2.2 copy.70
  24.7 2.2 copy.69
  27.7 1.8 fusion.20
  30.5 99.5 %all-reduce.13.cloned.1.call-done = (bf16[2,4,64,768]{3,2,1,0:T(8,128)(2,1)}, bf16[2,4,64,768]{3,2,1,0:T(8,128)(2,1)}) async-done(((bf16[2,4,64,768]{3,2,1,0:T(8,128)(2,1)}, bf16[2,4,64,768]{3,2,1,0:T(8,128)(2,1)}), (bf16[2,4,64,768]{3,2,1,0:T(8,128)(2,1)}, bf16[2,4,64,768]{3,2,1,0:T(8,128)(2,1)})) %all-reduce.13.cloned.1.call-update) | async-done | bytes 1572880 | tf_op jit(solution)/shard_map/psum | solution.py:16
  130.0 1.3 constant_dynamic-update-slice_fusion.1
  131.3 1.2 constant_dynamic-update-slice_fusion
  133.6 1.7 convolution_convert_fusion.1
  135.3 2.3 copy.49
  137.6 4.1 fusion.18
  141.7 48.8 %pmax.7 = f32[4,16,128]{2,1,0:T(8,128)} all-reduce(f32[4,16,128]{2,1,0:T(8,128)} %get-tuple-element.24), channel_id=1, replica_groups=mesh['samp'=2,'row'=8,'col'=16] {'col'}, use_global_device_ids=true, to_apply=%region_7.8 | all-reduce | flops 8192 | bytes 65536 | tf_op jit(solution)/shard_map/pmax | solution.py:99
  190.5 3.8 fusion.37
  194.3 3.0 copy.57
  197.5 3.7 multiply_convert_fusion
  201.1 2.3 copy.54
  203.4 3.0 fusion.63
  206.4 46.9 %psum.72 = f32[4,16,128]{2,1,0:T(8,128)} all-reduce(f32[4,16,128]{2,1,0:T(8,128)} %fusion.63), channel_id=1, replica_groups=mesh['samp'=2,'row'=8,'col'=16] {'col'}, use_global_device_ids=true, to_apply=%region_9.10 | all-reduce | flops 8192 | bytes 65536 | tf_op jit(solution)/shard_map/psum | solution.py:107
  253.4 56.6 %all-reduce.7.cloned.1.call-done = f32[4,128,768]{2,1,0:T(8,128)} async-done(((f32[4,128,768]{2,1,0:T(8,128)}), f32[4,128,768]{2,1,0:T(8,128)}) %all-reduce.7.cloned.1.call-update) | async-done | bytes 1572880 | tf_op jit(solution)/shard_map/psum | solution.py:107
  310.0 3.0 copy.58
  313.0 2.1 multiply_reduce_fusion
  315.3 3.6 fusion.66
  318.9 1.7 convolution_multiply_fusion.1
  320.6 3.1 copy.60
  323.7 5.6 broadcast_in_dim.13
  329.4 1.3 constant_dynamic-update-slice_fusion.2
  331.6 1.7 constant_dynamic-slice_fusion
  333.3 2.8 copy.71
  336.1 4.0 fusion.35
  340.1 2.8 copy.62
  342.9 2.5 fusion.44
  346.8 3.3 convolution_multiply_fusion
  350.1 2.8 copy.61
  352.9 3.4 convolution_select_fusion
  356.3 54.2 %reduce-scatter.2.cloned.1.call-done = f32[4,64,768]{2,1,0:T(8,128)} async-done(((f32[4,1024,768]{2,1,0:T(8,128)}), f32[4,64,768]{2,1,0:T(8,128)}) %reduce-scatter.2.cloned.1.call-update) | async-done | bytes 786448 | tf_op jit(solution)/shard_map/reduce_scatter | solution.py:148
  410.5 41.1 %all-reduce.9.cloned.1.call-done = f32[16,128,64]{1,0,2:T(8,128)} async-done(((f32[16,128,64]{1,0,2:T(8,128)}), f32[16,128,64]{1,0,2:T(8,128)}) %all-reduce.9.cloned.1.call-update) | async-done | bytes 524304 | tf_op jit(solution)/shard_map/psum | solution.py:165
  451.6 3.8 fusion.64
  455.4 2.8 fusion.12
  458.2 4.1 copy.66
  462.3 4.6 fusion.32
  466.9 336.1 %psum.79 = f32[128,16]{0,1:T(8,128)S(1)} all-reduce(f32[128,16]{0,1:T(8,128)S(1)} %fusion.32), channel_id=1, replica_groups=mesh['samp'=2,'row'=8,'col'=16] {'row','col'}, use_global_device_ids=true, to_apply=%region_23.24 | all-reduce | flops 2048 | bytes 16384 | tf_op jit(solution)/shard_map/psum | solution.py:169
  803.6 2.7 fusion.27
  806.4 2.5 convolution_add_fusion.1
  809.0 1.4 fusion.65
  (67 shorter events, 11.3 us)
Async XLA Ops:
  7.2 190.3 %copy-start = (bf16[768,768]{1,0:T(8,128)(2,1)S(1)}, bf16[768,768]{1,0:T(8,128)(2,1)}, u32[]{:S(2)}) copy-start(bf16[768,768]{1,0:T(8,128)(2,1)} %param.20) | copy-start | bytes 3538948
  7.2 4.8 copy-start.15
  7.2 122.8 %all-reduce.13.cloned.1.call-start = ((), (), s32[]{:S(2)}) async-start(), calls=%async_computation.5 | async-start | bytes 3145728 | tf_op jit(solution)/shard_map/psum | solution.py:16
  12.0 1.4 copy-start.2
  13.3 2.7 copy-start.8
  13.3 296.7 %all-reduce.7.cloned.1.call-start = ((), (), s32[]{:S(2)}) async-start(), calls=%async_computation.1 | async-start | bytes 3145728 | tf_op jit(solution)/shard_map/psum | solution.py:107
  21.1 6.6 copy-start.18
  26.9 3.6 copy-start.19
  130.0 3.6 copy-start.9
  132.5 1.2 copy-start.7
  197.4 213.1 %reduce-scatter.2.cloned.1.call-start = ((), (), s32[]{:S(2)}) async-start(), calls=%async_computation.2 | async-start | bytes 13369344 | tf_op jit(solution)/shard_map/reduce_scatter | solution.py:148
  313.0 2.3 copy-start.1
  313.0 2.3 copy-start.16
  313.0 2.3 copy-start.17
  315.3 3.6 copy-start.4
  318.9 1.7 copy-start.6
  323.7 5.6 copy-start.5
  330.7 120.9 %all-reduce.9.cloned.1.call-start = ((), (), s32[]{:S(2)}) async-start(), calls=%async_computation.3 | async-start | bytes 1048576 | tf_op jit(solution)/shard_map/psum | solution.py:165
  342.9 2.5 copy-start.14
  346.5 457.1 %all-reduce.11.cloned.1.call-start = ((), (), s32[]{:S(2)}) async-start(), calls=%async_computation.4 | async-start | bytes 6291456 | tf_op jit(solution)/shard_map/psum | solution.py:154
  803.6 2.7 copy-start.13
  806.3 2.6 copy-start.3
  806.3 2.6 copy-start.10
  806.3 2.6 copy-start.11
  806.3 2.6 copy-start.12
Sparse Core Ops, SparseCore 0:
  13.4 116.5 all-reduce.12
  197.5 112.4 all-reduce.6
  330.8 79.5 reduce-scatter.1
  412.9 38.6 all-reduce.8
  454.6 106.1 all-reduce.10
where the time goes:
time: 819 us; the launch traced here: 818 us
  blocking collectives  432 us (53%)
  waiting for transfers between devices  252 us (31%)
  matrix products  51.1 us (6%)
  local copies, waits for them, and re-layouts  49.3 us (6%)
  other arithmetic  19.6 us (2%)
  between operations  14.1 us (2%)
    psum x1, blocking collectives, body(): weight_sum = lax.psum(weight_part, ('row', 'col'))  336 us
    psum x1, waiting for transfers between devices, broadcast(): return lax.psum(block, axis)  99.5 us
    psum x1, waiting for transfers between devices, body(): lax.psum((jnp.sum(expo, axis=-1), partial_out.reshape(samp_dev, row_count...  56.6 us
    reduce_scatter x1, waiting for transfers between devices, body(): lax.psum_scatter(lax.dynamic_update_slice_in_dim(blank, grad_query, row_i...  54.2 us
    pmax x1, blocking collectives, body(): top = lax.pmax(jnp.max(scores, axis=-1), 'col')  48.8 us
    psum x1, blocking collectives, body(): lax.psum((jnp.sum(expo, axis=-1), partial_out.reshape(samp_dev, row_count...  46.9 us
    psum x1, waiting for transfers between devices, body(): grad_bias = lax.psum(bias_local, 'samp')  41.1 us
  transfers between devices with their start and end apart: 5, of which 4 were waited for; matrix products, arithmetic and copies ran while one was open for 8% of the time, Pallas kernels for 0%

commit v1 on v0

v1 whole, which is shorter than its diff:
```python
import functools
import math

import jax
import jax.numpy as jnp
from jax import lax
from jax.experimental import pallas as pl
from jax.experimental.pallas import tpu as pltpu
from jax.sharding import PartitionSpec as P

D = 768
H = 16
CH = 48
C = 128
NTYPE = 32
GROUP = 4
NG = H // GROUP
GW = GROUP * CH
EPS = 1e-05
NEG = -1000000000.0
BF = jnp.bfloat16
F32 = jnp.float32
MESH = pl.DeviceIdType.MESH


def dot_nn(a, b):
    return jnp.dot(a, b, preferred_element_type=F32)


def dot_nt(a, b):
    return lax.dot_general(a, b, (((1,), (1,)), ((), ())), preferred_element_type=F32)


def dot_tn(a, b):
    return lax.dot_general(a, b, (((0,), (0,)), ((), ())), preferred_element_type=F32)


def split(x):
    high = x.astype(BF)
    return high, (x - high.astype(F32)).astype(BF)


def norm(x):
    centred = x - jnp.mean(x, axis=-1, keepdims=True)
    inv = lax.rsqrt(jnp.mean(centred * centred, axis=-1, keepdims=True) + EPS)
    return centred * inv, inv


def norm_back(grad, normed, inv):
    return inv * (
        grad
        - jnp.mean(grad, axis=-1, keepdims=True)
        - normed * jnp.mean(grad * normed, axis=-1, keepdims=True)
    )


def kernel(
    sizes,
    tok_ref,
    rest_ref,
    table_ref,
    mask_ref,
    wbt_ref,
    cot_ref,
    wq_hbm,
    wk_hbm,
    wv_hbm,
    wg_hbm,
    pair_hbm,
    tg_ref,
    bw_ref,
    pg_hbm,
    wq_ref,
    wk_ref,
    wv_ref,
    wg_ref,
    pair_ref,
    raw_ref,
    nrm_ref,
    inv_ref,
    bias_ref,
    emb_ref,
    act_ref,
    k_ref,
    v_ref,
    sig_ref,
    qgs_ref,
    qg_ref,
    bdm_ref,
    keep_ref,
    e_ref,
    dp_ref,
    ot_ref,
    st_ref,
    str_ref,
    res_ref,
    resr_ref,
    gb_ref,
    gbr_ref,
    dkv_ref,
    ekv_ref,
    od_ref,
    ods_ref,
    dqs_ref,
    dqr_ref,
    os_ref,
    or_ref,
    pm_ref,
    pmr_ref,
    wg_acc_ref,
    hr_ref,
    hs_ref,
    hr2_ref,
    w_sem,
    pair_sem,
    out_sem,
    t_sem,
    ag_send,
    ag_recv,
    sib_send,
    sib_recv,
    b_send,
    b_recv,
    b2_send,
    b2_recv,
    e_send,
    e_recv,
    x_send,
    x_recv,
    d_send,
    d_recv,
    o_send,
    o_recv,
    f_sem,
    pm_sem,
    g_send,
    g_recv,
    h_send,
    h_recv,
    h2_send,
    h2_recv,
):
    n_row, n_col, total_tokens, samples = sizes
    samp = lax.axis_index("samp")
    row = lax.axis_index("row")
    col = lax.axis_index("col")
    core = lax.rem(col, 2)
    z = col // 2
    n_z = n_col // 2
    scale = 1.0 / math.sqrt(CH)
    rest_row = row // 2
    own_tok = pl.multiple_of(lax.rem(row, 2) * 32, 32)

    def at_col(c):
        return (samp, row, c)

    def at_row(r):
        return (samp, r, col)

    sibling = at_col(z * 2 + 1 - core)
    swapped = (samp, z, row * 2 + core)
    is_diag = row == z
    other_samp = (1 - samp, row, col)

    def remote(src, dst, send, recv, device):
        return pltpu.make_async_remote_copy(
            src_ref=src,
            dst_ref=dst,
            send_sem=send,
            recv_sem=recv,
            device_id=device,
            device_id_type=MESH,
        )

    weights = [
        pltpu.make_async_copy(src, dst, w_sem.at[n])
        for n, (src, dst) in enumerate(
            ((wq_hbm, wq_ref), (wg_hbm, wg_ref), (wk_hbm, wk_ref), (wv_hbm, wv_ref))
        )
    ]
    for copy in weights:
        copy.start()
    pair_copy = pltpu.make_async_copy(pair_hbm, pair_ref, pair_sem)
    pair_copy.start()

    barrier = pltpu.get_barrier_semaphore()

    def greet(device):
        pl.semaphore_signal(barrier, inc=1, device_id=device, device_id_type=MESH)

    def greet_col(d, carry):
        greet(at_col(lax.rem(col + d, n_col)))
        return carry

    def greet_row(d, carry):
        greet(at_row(lax.rem(row + d, n_row)))
        return carry

    lax.fori_loop(1, n_col, greet_col, 0)
    lax.fori_loop(1, n_row, greet_row, 0)
    greet(other_samp)

    @pl.when(jnp.logical_not(is_diag))
    def _():
        greet(swapped)

    onehot = (rest_ref[...] == lax.broadcasted_iota(jnp.int32, (64, NTYPE), 1)).astype(F32)
    emb_ref[...] = dot_nn(onehot.astype(BF), table_ref[...])
    own_rows = pl.ds(own_tok, 32)
    own_normed, own_inv = norm(tok_ref[rest_row, own_rows, :].astype(F32) + emb_ref[own_rows, :])
    own_act = own_normed.astype(BF)
    weights[0].wait()
    qgs_ref[0] = dot_nn(own_act, wq_ref[...]).astype(BF)
    weights[1].wait()
    gate = dot_nn(own_act, wg_ref[...]).astype(BF).astype(F32)
    sig = jax.nn.sigmoid(gate)
    sig_ref[...] = sig
    own_cot = cot_ref[rest_row, own_rows, :].astype(F32)
    qgs_ref[1] = (own_cot * sig).astype(BF)

    @pl.when(is_diag)
    def _():
        pl.semaphore_wait(barrier, n_col + n_row - 1)

    @pl.when(jnp.logical_not(is_diag))
    def _():
        pl.semaphore_wait(barrier, n_col + n_row)

    def region(zz, kk):
        start = pl.multiple_of(kk * 64 + lax.rem(zz, 2) * 32, 32)
        return qg_ref.at[zz // 2, :, pl.ds(start, 32), :]

    to_swapped = remote(qgs_ref, region(row, core), t_sem.at[0], t_sem.at[1], swapped)
    from_swapped = remote(qgs_ref, region(z, core), t_sem.at[0], t_sem.at[1], swapped)
    keep_own = pltpu.make_async_copy(qgs_ref, region(z, core), t_sem.at[2])

    @pl.when(jnp.logical_not(is_diag))
    def _():
        to_swapped.start()

    @pl.when(is_diag)
    def _():
        keep_own.start()

    weights[2].wait()
    weights[3].wait()

    def project(s, carry):
        normed, _ = norm(tok_ref[s].astype(F32) + emb_ref[...])
        act = normed.astype(BF)
        k_ref[s] = dot_nn(act, wk_ref[...]).astype(BF)
        v_ref[s] = dot_nn(act, wv_ref[...]).astype(BF)
        return carry

    lax.fori_loop(0, 4, project, 0)
    lane = lax.broadcasted_iota(jnp.int32, (64, GW), 1)
    for h in range(GROUP):
        inside = jnp.logical_and(lane >= h * CH, lane < (h + 1) * CH)
        bdm_ref[h * 64 : (h + 1) * 64, :] = jnp.where(inside, 1.0, 0.0).astype(BF)
    keep_ref[...] = jnp.where(mask_ref[...] == 1, 1.0, 0.0) * jnp.ones((64, 128), F32)

    @pl.when(jnp.logical_not(is_diag))
    def _():
        to_swapped.wait_send()
        from_swapped.wait_recv()

    @pl.when(is_diag)
    def _():
        keep_own.wait()

    def ag_copy(d):
        zz = lax.rem(z + d, n_z)
        return remote(
            region(z, core), region(z, core), ag_send.at[d], ag_recv.at[z], at_col(zz * 2 + core)
        )

    def ag_wait(zz):
        return remote(
            region(zz, core), region(zz, core), ag_send.at[0], ag_recv.at[zz], sibling
        )

    def sib_copy(zz):
        return remote(
            region(zz, core), region(zz, core), sib_send.at[zz], sib_recv.at[zz], sibling
        )

    def sib_wait(zz):
        return remote(
            region(zz, 1 - core), region(zz, 1 - core), sib_send.at[zz], sib_recv.at[zz], sibling
        )

    def order(t):
        near = (t + 1) // 2
        return jnp.where(lax.rem(t, 2) == 1, near, n_z - near)

    def ag_start(t, carry):
        ag_copy(order(t)).start()
        return carry

    lax.fori_loop(1, n_z, ag_start, 0)
    sib_copy(z).start()

    pair_copy.wait()

    def widen(n, carry):
        raw_ref[pl.ds(pl.multiple_of(n * 512, 512), 512), :] = (
            pair_ref[pl.ds(n * 8, 8)].astype(F32).reshape(512, C)
        )
        return carry

    lax.fori_loop(0, 16, widen, 0)
    wbt = wbt_ref[...]
    wbt_wide = jnp.concatenate([wbt, wbt], axis=1)

    def pair_forward(j, carry):
        normed, inv = norm(raw_ref[pl.ds(j, 128, stride=64), :])
        nrm_ref[j] = normed
        inv_ref[j] = jnp.broadcast_to(inv, (128, C))
        high, low = split(normed)
        both = jnp.concatenate([high, low], axis=1)
        bias_ref[pl.ds(j, H, stride=64), :] = dot_nt(wbt_wide, both)
        return carry

    def gather_step(t, carry):
        lax.fori_loop(t * 8, t * 8 + 8, pair_forward, 0)

        @pl.when(t > 0)
        def _():
            zz = lax.rem(z + n_z - order(t), n_z)
            ag_wait(zz).wait_recv()
            sib_copy(zz).start()

        return carry

    lax.fori_loop(0, n_z, gather_step, 0)

    def sib_arrive(zz, carry):
        sib_wait(zz).wait_recv()
        return carry

    lax.fori_loop(0, n_z, sib_arrive, 0)

    def blocks(ref, s, g):
        one = ref[s, :, g * GW : (g + 1) * GW]
        return jnp.concatenate([one] * GROUP, axis=0) * bdm_ref[...]

    def forward(s, carry):
        keep = jnp.broadcast_to(keep_ref[...][None], (GROUP, 64, 128)) > 0.5
        for g in range(NG):
            sg = s * NG + g
            key_b = blocks(k_ref, s, g)
            value_b = blocks(v_ref, s, g)
            query = qg_ref[s, 0, :, g * GW : (g + 1) * GW]
            gout = qg_ref[s, 1, :, g * GW : (g + 1) * GW]
            scores = dot_nt(key_b, query) * scale + bias_ref[g * 256 : (g + 1) * 256, :]
            scores = jnp.where(keep, scores.reshape(GROUP, 64, 128), NEG)
            top = jnp.max(scores, axis=1)
            expo = jnp.exp(scores - top[:, None, :])
            expo_b = expo.astype(BF)
            pre = dot_nt(value_b, gout).reshape(GROUP, 64, 128)
            st_ref[sg, 0:4, :] = top
            st_ref[sg, 4:8, :] = jnp.sum(expo, axis=1)
            st_ref[sg, 8:12, :] = jnp.sum(expo_b.astype(F32) * pre, axis=1)
            st_ref[sg, 12:16, :] = top
            e_ref[sg] = expo.reshape(256, 128)
            dp_ref[sg] = pre.reshape(256, 128)
            ot_ref[s, g * GW : (g + 1) * GW, :] = dot_tn(value_b, expo_b.reshape(256, 128))
        return carry

    lax.fori_loop(0, 4, forward, 0)

    def b_copy(d):
        c = lax.rem(col + d, n_col)
        return remote(st_ref.at[c], str_ref.at[col], b_send.at[d], b_recv.at[col], at_col(c))

    def b_wait(d):
        c = lax.rem(col + n_col - d, n_col)
        return remote(st_ref.at[c], str_ref.at[c], b_send.at[d], b_recv.at[c], at_col(c))

    def b2_copy(d):
        c = lax.rem(col + d, n_col)
        return remote(res_ref, resr_ref.at[col], b2_send.at[d], b2_recv.at[col], at_col(c))

    def b2_wait(d):
        c = lax.rem(col + n_col - d, n_col)
        return remote(res_ref, resr_ref.at[c], b2_send.at[d], b2_recv.at[c], at_col(c))

    def start_all(make, count):
        def step(d, carry):
            make(d).start()
            return carry

        lax.fori_loop(1, count, step, 0)

    def recv_all(make, count):
        def step(d, carry):
            make(d).wait_recv()
            return carry

        lax.fori_loop(1, count, step, 0)

    def sent_all(make, count):
        def step(d, carry):
            make(d).wait_send()
            return carry

        lax.fori_loop(1, count, step, 0)

    start_all(b_copy, n_col)
    str_ref[col] = st_ref[col]
    recv_all(b_wait, n_col)
    parts = str_ref[...]
    tops = parts[:, 0:4, :]
    top_all = jnp.max(tops, axis=0)
    weight = jnp.exp(tops - top_all[None])
    inv_total = 1.0 / jnp.sum(parts[:, 4:8, :] * weight, axis=0)
    delta = jnp.sum(parts[:, 8:12, :] * weight, axis=0) * inv_total
    res_ref[0:4, :] = top_all
    res_ref[4:8, :] = inv_total
    res_ref[8:12, :] = delta
    res_ref[12:16, :] = delta
    resr_ref[col] = res_ref[...]
    start_all(b2_copy, n_col)
    recv_all(b2_wait, n_col)

    def e_copy(r):
        start = pl.multiple_of(lax.rem(r, 2) * 32, 32)
        return remote(
            dkv_ref.at[r // 2, :, pl.ds(start, 32), :],
            ekv_ref.at[row],
            e_send.at[r],
            e_recv.at[row],
            at_row(r),
        )

    def e_wait(d):
        r = lax.rem(row + n_row - d, n_row)
        return remote(
            dkv_ref.at[0, :, pl.ds(0, 32), :],
            ekv_ref.at[r],
            e_send.at[r],
            e_recv.at[r],
            at_row(r),
        )

    my_half = pl.multiple_of(core * 64, 64)
    their_half = pl.multiple_of((1 - core) * 64, 64)

    def x_copy(s):
        return remote(
            od_ref.at[s, :, pl.ds(their_half, 64), :],
            ods_ref.at[s],
            x_send.at[s],
            x_recv.at[s],
            sibling,
        )

    gb_ref[...] = jnp.zeros_like(gb_ref)
    lane4 = lax.broadcasted_iota(jnp.int32, (64, GW), 1)

    def diagonal(full):
        picked = full[3 * 64 : 4 * 64]
        for h in (2, 1, 0):
            picked = jnp.where(lane4 < (h + 1) * CH, full[h * 64 : (h + 1) * 64], picked)
        return picked

    def backward(t, carry):
        s = lax.rem(t + rest_row, 4)
        keys, values, queries, outs = [], [], [], []
        for g in range(NG):
            sg = s * NG + g
            factor = jnp.exp(st_ref[sg, 0:4, :] - resr_ref[sg, 0:4, :]) * resr_ref[sg, 4:8, :]
            down = resr_ref[sg, 8:12, :]
            probs = e_ref[sg].reshape(GROUP, 64, 128) * factor[:, None, :]
            grads = probs * (dp_ref[sg].reshape(GROUP, 64, 128) - down[:, None, :])
            grads = grads.reshape(256, 128)
            gb_ref[g] += grads
            grads_b = grads.astype(BF)
            probs_b = probs.reshape(256, 128).astype(BF)
            query = qg_ref[s, 0, :, g * GW : (g + 1) * GW]
            gout = qg_ref[s, 1, :, g * GW : (g + 1) * GW]
            keys.append(diagonal(dot_nn(grads_b, query)) * scale)
            values.append(diagonal(dot_nn(probs_b, gout)))
            queries.append(dot_tn(grads_b, blocks(k_ref, s, g)) * scale)
            part = ot_ref[s, g * GW : (g + 1) * GW, :].reshape(GROUP, CH, 128)
            outs.append((part * factor[:, None, :]).reshape(GW, 128).T)
        dkv_ref[s, 0] = jnp.concatenate(keys, axis=1)
        dkv_ref[s, 1] = jnp.concatenate(values, axis=1)
        od_ref[s, 0] = jnp.concatenate(outs, axis=1)
        od_ref[s, 1] = jnp.concatenate(queries, axis=1)
        x_copy(s).start()
        for half in range(2):
            r = s * 2 + half

            @pl.when(r != row)
            def _():
                e_copy(r).start()

        return carry

    lax.fori_loop(0, 4, backward, 0)

    bias_copy = remote(gb_ref, gbr_ref, f_sem.at[0], f_sem.at[1], other_samp)
    bias_copy.start()

    def d_copy(zz):
        rows = pl.ds(pl.multiple_of(lax.rem(zz, 2) * 32, 32), 32)
        return remote(
            dqs_ref.at[zz // 2, rows, :],
            dqr_ref.at[z],
            d_send.at[zz],
            d_recv.at[z],
            at_col(zz * 2 + core),
        )

    def o_copy(zz):
        rows = pl.ds(pl.multiple_of(lax.rem(zz, 2) * 32, 32), 32)
        return remote(
            os_ref.at[zz // 2, rows, :],
            or_ref.at[z],
            o_send.at[zz],
            o_recv.at[z],
            at_col(zz * 2 + core),
        )

    def zz_wait(make_dst, sem_send, sem_recv):
        def make(d):
            zz = lax.rem(z + n_z - d, n_z)
            return remote(
                make_dst.at[zz], make_dst.at[zz], sem_send.at[zz], sem_recv.at[zz], sibling
            )

        return make

    def spread(t, carry):
        s = lax.rem(t + rest_row, 4)
        x_copy(s).wait_recv()
        os_ref[s] = (od_ref[s, 0, pl.ds(my_half, 64), :] + ods_ref[s, 0]).astype(BF)
        dqs_ref[s] = od_ref[s, 1, pl.ds(my_half, 64), :] + ods_ref[s, 1]
        for half in range(2):
            zz = s * 2 + half

            @pl.when(zz != z)
            def _():
                d_copy(zz).start()
                o_copy(zz).start()

        return carry

    lax.fori_loop(0, 4, spread, 0)
    z_rows = pl.ds(pl.multiple_of(lax.rem(z, 2) * 32, 32), 32)
    dqr_ref[z] = dqs_ref[z // 2, z_rows, :]
    or_ref[z] = os_ref[z // 2, z_rows, :]

    bias_copy.wait_recv()
    wg_acc_ref[...] = jnp.zeros_like(wg_acc_ref)
    wbt_tall = jnp.concatenate([wbt, wbt], axis=0)
    pair_scale = total_tokens / samples

    def pair_backward(j, carry):
        grad = bias_ref[pl.ds(j, H, stride=64), :]
        high, low = split(grad)
        grad_hl = jnp.concatenate([high, low], axis=0)
        normed = nrm_ref[j]
        n_high, n_low = split(normed)
        wg_acc_ref[...] += dot_nn(grad_hl, jnp.concatenate([n_high, n_low], axis=1))
        back = norm_back(dot_tn(grad_hl, wbt_tall), normed, inv_ref[j])
        raw_ref[pl.ds(j, 128, stride=64), :] = back * pair_scale
        return carry

    bias_ref[...] = gb_ref[...].reshape(H * 64, 128) + gbr_ref[...].reshape(H * 64, 128)
    lax.fori_loop(0, 64, pair_backward, 0)

    def weight_copy(d):
        c = lax.rem(col + d, n_col)
        return remote(hs_ref.at[0], hr_ref.at[col], h_send.at[d], h_recv.at[col], at_col(c))

    def weight_wait(d):
        c = lax.rem(col + n_col - d, n_col)
        return remote(hs_ref.at[0], hr_ref.at[c], h_send.at[d], h_recv.at[c], at_col(c))

    acc = wg_acc_ref[...]
    hs_ref[0] = (acc[0:H, 0:C] + acc[H:, 0:C]) + (acc[0:H, C:] + acc[H:, C:])
    start_all(weight_copy, n_col)
    hr_ref[col] = hs_ref[0]

    recv_all(zz_wait(dqr_ref, d_send, d_recv), n_z)
    recv_all(zz_wait(or_ref, o_send, o_recv), n_z)
    pm_ref[0] = jnp.sum(or_ref[...].astype(F32), axis=0)
    pm_ref[1] = jnp.sum(dqr_ref[...], axis=0)
    pm_copy = remote(pm_ref, pmr_ref, pm_sem.at[0], pm_sem.at[1], swapped)
    pm_own = pltpu.make_async_copy(pm_ref, pmr_ref, pm_sem.at[2])

    @pl.when(jnp.logical_not(is_diag))
    def _():
        pm_copy.start()

    @pl.when(is_diag)
    def _():
        pm_own.start()

    def narrow(n, carry):
        pair_ref[pl.ds(n * 8, 8)] = (
            raw_ref[pl.ds(pl.multiple_of(n * 512, 512), 512), :].reshape(8, 64, C).astype(BF)
        )
        return carry

    lax.fori_loop(0, 16, narrow, 0)
    out_copy = pltpu.make_async_copy(pair_ref, pg_hbm, out_sem)
    out_copy.start()

    recv_all(weight_wait, n_col)
    hs_ref[1] = jnp.sum(hr_ref[...], axis=0)

    def weight2_copy(d):
        r = lax.rem(row + d, n_row)
        return remote(hs_ref.at[1], hr2_ref.at[row], h2_send.at[d], h2_recv.at[row], at_row(r))

    def weight2_wait(d):
        r = lax.rem(row + n_row - d, n_row)
        return remote(hs_ref.at[1], hr2_ref.at[r], h2_send.at[d], h2_recv.at[r], at_row(r))

    start_all(weight2_copy, n_row)
    hr2_ref[row] = hs_ref[1]

    ekv_ref[row] = dkv_ref[rest_row, :, own_rows, :]
    recv_all(e_wait, n_row)
    grad_kv = jnp.sum(ekv_ref[...], axis=0)

    def back_project(grad, weight_ref):
        high, low = split(grad)
        both = dot_nt(jnp.concatenate([high, low], axis=0), weight_ref[...])
        return both[0:32] + both[32:64]

    total = back_project(grad_kv[0], wk_ref) + back_project(grad_kv[1], wv_ref)

    @pl.when(jnp.logical_not(is_diag))
    def _():
        pm_copy.wait()

    @pl.when(is_diag)
    def _():
        pm_own.wait()

    total = total + back_project(pmr_ref[1], wq_ref)
    own_sig = sig_ref[...]
    cot = cot_ref[rest_row, own_rows, :].astype(F32)
    grad_gate = (cot * pmr_ref[0] * own_sig * (1.0 - own_sig)).astype(BF)
    total = total + dot_nt(grad_gate, wg_ref[...])
    own_normed, own_inv = norm(tok_ref[rest_row, own_rows, :].astype(F32) + emb_ref[own_rows, :])
    tg_ref[rest_row, own_rows, :] = norm_back(total, own_normed, own_inv).astype(BF)

    def g_copy(d):
        r = lax.rem(row + d, n_row)
        mine = tg_ref.at[rest_row, own_rows, :]
        return remote(mine, mine, g_send.at[d], g_recv.at[row], at_row(r))

    def g_wait(d):
        r = lax.rem(row + n_row - d, n_row)
        start = pl.multiple_of(lax.rem(r, 2) * 32, 32)
        theirs = tg_ref.at[r // 2, pl.ds(start, 32), :]
        return remote(theirs, theirs, g_send.at[d], g_recv.at[r], at_row(r))

    start_all(g_copy, n_row)
    recv_all(weight2_wait, n_row)
    bw_ref[...] = jnp.sum(hr2_ref[...], axis=0) * (1.0 / samples)

    sent_all(ag_copy, n_z)
    sent_all(b_copy, n_col)
    sent_all(b2_copy, n_col)
    sent_all(weight_copy, n_col)
    sent_all(weight2_copy, n_row)
    bias_copy.wait_send()

    def left(n, carry):
        sib_copy(n).wait_send()

        @pl.when(n != row)
        def _():
            e_copy(n).wait_send()

        @pl.when(n != z)
        def _():
            d_copy(n).wait_send()
            o_copy(n).wait_send()

        return carry

    lax.fori_loop(0, n_z, left, 0)

    def left_x(s, carry):
        x_copy(s).wait_send()
        return carry

    lax.fori_loop(0, 4, left_x, 0)
    recv_all(g_wait, n_row)
    sent_all(g_copy, n_row)
    out_copy.wait()


def body(
    tokens, restype, type_table, key_mask, pair, w_bias, w_query, w_key, w_value, w_gate, cotangent
):
    n_row = lax.axis_size("row")
    n_col = lax.axis_size("col")
    n_z = n_col // 2
    samples = tokens.shape[0] * lax.axis_size("samp")
    total_tokens = tokens.shape[1] * n_col
    vmem = pl.BlockSpec(memory_space=pltpu.VMEM)
    hbm = pl.BlockSpec(memory_space=pl.ANY)
    dma = pltpu.SemaphoreType.DMA
    token_grad, weight_grad, pair_grad = pl.pallas_call(
        functools.partial(kernel, (n_row, n_col, total_tokens, samples)),
        out_shape=(
            jax.ShapeDtypeStruct((4, 64, D), BF),
            jax.ShapeDtypeStruct((H, C), F32),
            jax.ShapeDtypeStruct((128, 64, C), BF),
        ),
        in_specs=[vmem] * 6 + [hbm] * 5,
        out_specs=(vmem, vmem, hbm),
        scratch_shapes=[
            pltpu.VMEM((D, D), BF),
            pltpu.VMEM((D, D), BF),
            pltpu.VMEM((D, D), BF),
            pltpu.VMEM((D, D), BF),
            pltpu.VMEM((128, 64, C), BF),
            pltpu.VMEM((8192, C), F32),
            pltpu.VMEM((64, 128, C), F32),
            pltpu.VMEM((64, 128, C), F32),
            pltpu.VMEM((H * 64, 128), F32),
            pltpu.VMEM((64, D), F32),
            pltpu.VMEM((16, 128), F32),
            pltpu.VMEM((4, 64, D), BF),
            pltpu.VMEM((4, 64, D), BF),
            pltpu.VMEM((32, D), F32),
            pltpu.VMEM((2, 32, D), BF),
            pltpu.VMEM((4, 2, 128, D), BF),
            pltpu.VMEM((256, GW), BF),
            pltpu.VMEM((64, 128), F32),
            pltpu.VMEM((16, 256, 128), F32),
            pltpu.VMEM((16, 256, 128), F32),
            pltpu.VMEM((4, D, 128), F32),
            pltpu.VMEM((16, 16, 128), F32),
            pltpu.VMEM((16, 16, 128), F32),
            pltpu.VMEM((16, 128), F32),
            pltpu.VMEM((16, 16, 128), F32),
            pltpu.VMEM((NG, 256, 128), F32),
            pltpu.VMEM((NG, 256, 128), F32),
            pltpu.VMEM((4, 2, 64, D), F32),
            pltpu.VMEM((n_row, 2, 32, D), F32),
            pltpu.VMEM((4, 2, 128, D), F32),
            pltpu.VMEM((4, 2, 64, D), F32),
            pltpu.VMEM((4, 64, D), F32),
            pltpu.VMEM((n_z, 32, D), F32),
            pltpu.VMEM((4, 64, D), BF),
            pltpu.VMEM((n_z, 32, D), BF),
            pltpu.VMEM((2, 32, D), F32),
            pltpu.VMEM((2, 32, D), F32),
            pltpu.VMEM((2 * H, 2 * C), F32),
            pltpu.VMEM((n_col, H, C), F32),
            pltpu.VMEM((2, H, C), F32),
            pltpu.VMEM((n_row, H, C), F32),
            dma((4,)),
            dma,
            dma,
            dma((3,)),
            dma((n_z,)),
            dma((n_z,)),
            dma((n_z,)),
            dma((n_z,)),
            dma((n_col,)),
            dma((n_col,)),
            dma((n_col,)),
            dma((n_col,)),
            dma((n_row,)),
            dma((n_row,)),
            dma((4,)),
            dma((4,)),
            dma((n_z,)),
            dma((n_z,)),
            dma((n_z,)),
            dma((n_z,)),
            dma((2,)),
            dma((3,)),
            dma((n_row,)),
            dma((n_row,)),
            dma((n_col,)),
            dma((n_col,)),
            dma((n_row,)),
            dma((n_row,)),
        ],
        compiler_params=pltpu.CompilerParams(
            collective_id=0, has_side_effects=True, vmem_limit_bytes=60 * 1024 * 1024
        ),
    )(
        tokens,
        restype.reshape(64, 1),
        type_table,
        key_mask.reshape(64, 1),
        w_bias.T,
        cotangent,
        w_query,
        w_key,
        w_value,
        w_gate,
        pair,
    )
    return (token_grad, pair_grad, weight_grad.T)


def solution(mesh):
    placed = (
        P("samp", "col", None),
        P("col"),
        P(),
        P("col"),
        P("row", "col", None),
        P(),
        P(),
        P(),
        P(),
        P(),
        P("samp", "col", None),
    )
    return jax.shard_map(
        body,
        mesh=mesh,
        in_specs=placed,
        out_specs=(P("samp", "col", None), P("row", "col", None), P()),
        check_vma=False,
    )
```

time: 819 us -> 164 us (0.20)
  blocking collectives: 432 us -> 0 us
  waiting for transfers between devices: 252 us -> 0 us
  Pallas kernels: 0 us -> 154 us
  matrix products: 51.1 us -> 0 us
  local copies, waits for them, and re-layouts: 49.3 us -> 8.18 us
  other arithmetic: 19.6 us -> 0 us
  between operations: 14.1 us -> 0.64 us
    psum x2 -> x0, blocking collectives: 383 us -> none  [the longest x1 336 us: body(): weight_sum = lax.psum(weight_part, ('row', 'col'))]
    psum x4 -> x0, waiting for transfers between devices: 197 us -> none  [the longest x1 99.5 us: broadcast(): return lax.psum(block, axis)]
    pallas_call x0 -> x1, Pallas kernels: none -> 154 us  [body(): pl.pallas_call(functools.partial(kernel, (n_row, n_col, total_tokens, sam...]
    reduce_scatter x1 -> x0, waiting for transfers between devices: 54.2 us -> none  [body(): lax.psum_scatter(lax.dynamic_update_slice_in_dim(blank, grad_query, row_i...]
    dot_general x18 -> x0, matrix products: 51.1 us -> none  [the longest x4 9.22 us: project(): jnp.einsum('std,de->ste', rows_in, weight, preferred_element_type=jnp.flo...]
    pmax x1 -> x0, blocking collectives: 48.8 us -> none  [body(): top = lax.pmax(jnp.max(scores, axis=-1), 'col')]
    reshape x6 -> x2, local copies, waits for them, and re-layouts: 16 us -> 2.72 us  [the longest x1 1.36 us: body(): restype.reshape(64, 1)]
    reduce_sum x6 -> x0, other arithmetic: 9.42 us -> none  [the longest x1 3.01 us: body(): jnp.sum(expo, axis=-1)]
  transfers between devices with their start and end apart: 5 -> 0, of which waited for: 4 -> 0; matrix products, arithmetic and copies ran while one was open for 8% -> 0% of each run, Pallas kernels for 0% -> 0%
where the time goes in v1:
time: 164 us; the launch traced here: 163 us
  Pallas kernels  154 us (94%)
  local copies, waits for them, and re-layouts  8.18 us (5%)
    pallas_call x1, Pallas kernels, body(): pl.pallas_call(functools.partial(kernel, (n_row, n_col, total_tokens, sam...  154 us
    unnamed x5, local copies, waits for them, and re-layouts  5.46 us

profile of v1, /device:TPU:8, one launch (start us, length us, event | category | flops | bytes accessed | tf_op | source)
XLA Modules:
  0.0 162.8 jit_solution(18064945468614885289)
XLA Ops:
  0.6 1.4 copy.14.rest_ref
  2.0 1.4 copy.15.mask_ref
  3.3 154.0 %shard_map.130 = (bf16[4,64,768]{2,1,0:T(8,128)(2,1)}, f32[16,128]{1,0:T(8,128)}, bf16[128,64,128]{2,1,0:T(8,128)(2,1)}) custom-call(bf16[4,64,768]{2,1,0:T(8,128)(2,1)} %tok_ref.1, s32[64,1]{1,0:T(8,128)} %copy.14.rest_ref, bf16[32,768]{1,0:T(8,128)(2,1)} %table_ref.1, s32[64,1]{1,0:T(8,128)} %copy.15.mask_ref, bf16[16,128]{1,0:T(8,128)(2,1)} %bitcast.5, ...), custom_call_target="tpu_custom_call" | custom-call | tf_op jit(solution)/shard_map/pallas_call | solution.py:712
  157.4 1.8 %copy.19 = bf16[4,64,768]{2,1,0:T(8,128)(2,1)} copy(bf16[4,64,768]{2,1,0:T(8,128)(2,1)} %get-tuple-element.12) | data formatting | bytes 786432
  159.1 0.0 copy-start
  159.1 3.1 %copy.20 = bf16[128,64,128]{2,1,0:T(8,128)(2,1)} copy(bf16[128,64,128]{2,1,0:T(8,128)(2,1)} %get-tuple-element.13) | data formatting | bytes 4194304
  162.2 0.0 copy-done
  162.2 0.6 copy.21
Async XLA Ops:
  159.1 3.1 %copy-start = (f32[16,128]{1,0:T(8,128)S(1)}, f32[16,128]{1,0:T(8,128)}, u32[]{:S(2)}) copy-start(f32[16,128]{1,0:T(8,128)} %get-tuple-element.8) | copy-start | bytes 24580

commit v2 on v1

v2 whole, which is shorter than its diff:
```python
import functools
import math

import jax
import jax.numpy as jnp
from jax import lax
from jax.experimental import pallas as pl
from jax.experimental.pallas import tpu as pltpu
from jax.sharding import PartitionSpec as P

D = 768
H = 16
CH = 48
C = 128
NTYPE = 32
GROUP = 4
NG = H // GROUP
GW = GROUP * CH
EPS = 1e-05
NEG = -1000000000.0
BF = jnp.bfloat16
F32 = jnp.float32
MESH = pl.DeviceIdType.MESH


def dot_nn(a, b):
    return jnp.dot(a, b, preferred_element_type=F32)


def dot_nt(a, b):
    return lax.dot_general(a, b, (((1,), (1,)), ((), ())), preferred_element_type=F32)


def dot_tn(a, b):
    return lax.dot_general(a, b, (((0,), (0,)), ((), ())), preferred_element_type=F32)


def split(x):
    high = x.astype(BF)
    return high, (x - high.astype(F32)).astype(BF)


def norm(x):
    centred = x - jnp.mean(x, axis=-1, keepdims=True)
    inv = lax.rsqrt(jnp.mean(centred * centred, axis=-1, keepdims=True) + EPS)
    return centred * inv, inv


def norm_back(grad, normed, inv):
    return inv * (
        grad
        - jnp.mean(grad, axis=-1, keepdims=True)
        - normed * jnp.mean(grad * normed, axis=-1, keepdims=True)
    )


def kernel(
    sizes,
    tok_ref,
    rest_ref,
    table_ref,
    mask_ref,
    wbt_ref,
    cot_ref,
    wq_hbm,
    wk_hbm,
    wv_hbm,
    wg_hbm,
    pair_hbm,
    tg_ref,
    bw_ref,
    pg_ref,
    wq_ref,
    wk_ref,
    wv_ref,
    wg_ref,
    pair_ref,
    raw_ref,
    nrm_ref,
    inv_ref,
    bias_ref,
    emb_ref,
    k_ref,
    v_ref,
    sig_ref,
    qgs_ref,
    qg_ref,
    bdm_ref,
    keep_ref,
    e_ref,
    dp_ref,
    ot_ref,
    st_ref,
    str_ref,
    res_ref,
    resr_ref,
    gbs_ref,
    gbr_ref,
    gr_ref,
    pr_ref,
    dkv_ref,
    ekv_ref,
    ey_ref,
    od_ref,
    ods_ref,
    dqs_ref,
    dqr_ref,
    pm_ref,
    pmr_ref,
    inner_ref,
    hr_ref,
    hs_ref,
    hr2_ref,
    w_sem,
    pair_sem,
    t_sem,
    ag_send,
    ag_recv,
    sib_send,
    sib_recv,
    b_send,
    b_recv,
    b2_send,
    b2_recv,
    e_send,
    e_recv,
    ey_sem,
    x_send,
    x_recv,
    d_send,
    d_recv,
    f_send,
    f_recv,
    pm_sem,
    g_send,
    g_recv,
    h_send,
    h_recv,
    h2_send,
    h2_recv,
):
    n_row, n_col, total_tokens, samples = sizes
    samp = lax.axis_index("samp")
    row = lax.axis_index("row")
    col = lax.axis_index("col")
    core = lax.rem(col, 2)
    z = col // 2
    n_z = n_col // 2
    scale = 1.0 / math.sqrt(CH)
    rest_row = row // 2
    own_tok = pl.multiple_of(lax.rem(row, 2) * 32, 32)

    def at_col(c):
        return (samp, row, c)

    def at_row(r):
        return (samp, r, col)

    sibling = at_col(z * 2 + 1 - core)

    def differ(a, b):
        return sum(lax.rem(a // bit + b // bit, 2) * bit for bit in (1, 2, 4))

    slice_here = differ(z, row)
    query_dev = (samp, z, slice_here * 2 + core)
    owner_dev = (samp, slice_here, row * 2 + core)
    is_self = row + z == 0
    other_samp = (1 - samp, row, col)

    def remote(src, dst, send, recv, device):
        return pltpu.make_async_remote_copy(
            src_ref=src,
            dst_ref=dst,
            send_sem=send,
            recv_sem=recv,
            device_id=device,
            device_id_type=MESH,
        )

    weights = [
        pltpu.make_async_copy(src, dst, w_sem.at[n])
        for n, (src, dst) in enumerate(
            ((wq_hbm, wq_ref), (wg_hbm, wg_ref), (wk_hbm, wk_ref), (wv_hbm, wv_ref))
        )
    ]
    for copy in weights:
        copy.start()
    pair_copy = pltpu.make_async_copy(pair_hbm, pair_ref, pair_sem)
    pair_copy.start()

    barrier = pltpu.get_barrier_semaphore()

    def greet(device):
        pl.semaphore_signal(barrier, inc=1, device_id=device, device_id_type=MESH)

    def greet_col(d, carry):
        greet(at_col(lax.rem(col + d, n_col)))
        return carry

    def greet_row(d, carry):
        greet(at_row(lax.rem(row + d, n_row)))
        return carry

    lax.fori_loop(1, n_col, greet_col, 0)
    lax.fori_loop(1, n_row, greet_row, 0)
    greet(other_samp)

    @pl.when(jnp.logical_not(is_self))
    def _():
        greet(query_dev)
        greet(owner_dev)

    onehot = jnp.where(rest_ref[...] == lax.broadcasted_iota(jnp.int32, (NTYPE, 64), 0), 1.0, 0.0)
    emb_ref[...] = dot_tn(onehot.astype(BF), table_ref[...])
    own_rows = pl.ds(own_tok, 32)
    own_normed, own_inv = norm(tok_ref[rest_row, own_rows, :].astype(F32) + emb_ref[own_rows, :])
    own_act = own_normed.astype(BF)
    weights[0].wait()
    qgs_ref[0] = dot_nn(own_act, wq_ref[...]).astype(BF)
    weights[1].wait()
    gate = dot_nn(own_act, wg_ref[...]).astype(BF).astype(F32)
    sig = jax.nn.sigmoid(gate)
    sig_ref[...] = sig
    own_cot = cot_ref[rest_row, own_rows, :].astype(F32)
    qgs_ref[1] = (own_cot * sig).astype(BF)

    weights[2].wait()
    weights[3].wait()

    def project(s, carry):
        normed, _ = norm(tok_ref[s].astype(F32) + emb_ref[...])
        act = normed.astype(BF)
        k_ref[s] = dot_nn(act, wk_ref[...]).astype(BF)
        v_ref[s] = dot_nn(act, wv_ref[...]).astype(BF)
        return carry

    lax.fori_loop(0, 4, project, 0)
    lane = lax.broadcasted_iota(jnp.int32, (64, GW), 1)
    for h in range(GROUP):
        inside = jnp.logical_and(lane >= h * CH, lane < (h + 1) * CH)
        bdm_ref[h * 64 : (h + 1) * 64, :] = jnp.where(inside, 1.0, 0.0).astype(BF)
    first_row = lax.broadcasted_iota(jnp.int32, (16, 64), 0) == 0
    kept = jnp.where(jnp.logical_and(mask_ref[...] == 1, first_row), 1.0, 0.0)
    keep_ref[...] = dot_tn(kept.astype(BF), jnp.ones((16, 128), BF))

    pair_copy.wait()

    def widen(n, carry):
        raw_ref[pl.ds(pl.multiple_of(n * 512, 512), 512), :] = (
            pair_ref[pl.ds(n * 8, 8)].astype(F32).reshape(512, C)
        )
        return carry

    lax.fori_loop(0, 16, widen, 0)
    @pl.when(is_self)
    def _():
        pl.semaphore_wait(barrier, n_col + n_row - 1)

    @pl.when(jnp.logical_not(is_self))
    def _():
        pl.semaphore_wait(barrier, n_col + n_row + 1)

    def region(number):
        start = pl.multiple_of(core * 64 + lax.rem(number, 2) * 32, 32)
        return qg_ref.at[number // 2, :, pl.ds(start, 32), :]

    to_swapped = remote(qgs_ref, region(row), t_sem.at[0], t_sem.at[1], query_dev)
    from_swapped = remote(qgs_ref, region(slice_here), t_sem.at[0], t_sem.at[1], owner_dev)
    keep_own = pltpu.make_async_copy(qgs_ref, region(slice_here), t_sem.at[2])

    @pl.when(jnp.logical_not(is_self))
    def _():
        to_swapped.start()

    @pl.when(is_self)
    def _():
        keep_own.start()

    @pl.when(jnp.logical_not(is_self))
    def _():
        to_swapped.wait_send()
        from_swapped.wait_recv()

    @pl.when(is_self)
    def _():
        keep_own.wait()

    def part_of(zz, kk, part):
        number = differ(zz, row)
        start = pl.multiple_of(kk * 64 + lax.rem(number, 2) * 32, 32)
        return qg_ref.at[number // 2, part, pl.ds(start, 32), :]

    def ag_copy(way, part, step):
        origin = lax.rem(z + n_z - way * step, n_z)
        mine = part_of(origin, core, part)
        sem = (part * 2 + (way + 1) // 2) * 4 + step
        there = at_col(lax.rem(z + n_z + way, n_z) * 2 + core)
        return remote(mine, mine, ag_send.at[sem], ag_recv.at[sem], there)

    def ag_wait(way, part, step):
        origin = lax.rem(z + 2 * n_z - way * (step + 1), n_z)
        mine = part_of(origin, core, part)
        sem = (part * 2 + (way + 1) // 2) * 4 + step
        return remote(mine, mine, ag_send.at[sem], ag_recv.at[sem], sibling)

    def sib_copy(zz, part):
        mine = part_of(zz, core, part)
        sem = zz * 2 + part
        return remote(mine, mine, sib_send.at[sem], sib_recv.at[sem], sibling)

    def sib_wait(zz, part):
        theirs = part_of(zz, 1 - core, part)
        sem = zz * 2 + part
        return remote(theirs, theirs, sib_send.at[sem], sib_recv.at[sem], sibling)

    def last_step(way, part):
        return 3 if (way == 1) == (part == 0) else 2

    for part in range(2):
        for way in (1, -1):
            ag_copy(way, part, 0).start()
        sib_copy(z, part).start()

    wbt = wbt_ref[...]
    wbt_wide = jnp.concatenate([wbt, wbt], axis=1)
    mean_one = jnp.full((C, C), 1.0 / C, BF)
    mean_two = jnp.full((2 * C, C), 1.0 / C, BF)

    def pair_forward(n, carry):
        first = n * 4
        values = jnp.concatenate(
            [raw_ref[pl.ds(first + u, 128, stride=64), :] for u in range(4)], axis=0
        )
        centred = values - dot_nn(values.astype(BF), mean_one)
        variance = dot_nn(jnp.concatenate(split(centred * centred), axis=1), mean_two)
        inv = lax.rsqrt(variance + EPS)
        normed = centred * inv
        nrm_ref[pl.ds(first, 4)] = normed.reshape(4, 128, C)
        inv_ref[pl.ds(first, 4)] = inv.reshape(4, 128, C)
        both = jnp.concatenate(split(normed), axis=1)
        for u in range(4):
            bias_ref[pl.ds(first + u, H, stride=64), :] = dot_nt(
                wbt_wide, both[u * 128 : (u + 1) * 128]
            )
        return carry

    def gather_step(step, carry):
        for part in range(2):
            for n in range(2):
                pair_forward(step * 4 + part * 2 + n, 0)
            for way in (1, -1):

                @pl.when(step <= last_step(way, part))
                def _():
                    ag_wait(way, part, step).wait_recv()

                @pl.when(step < last_step(way, part))
                def _():
                    ag_copy(way, part, step + 1).start()

                @pl.when(step <= last_step(way, part))
                def _():
                    sib_copy(lax.rem(z + 2 * n_z - way * (step + 1), n_z), part).start()

        return carry

    lax.fori_loop(0, 4, gather_step, 0)

    def sib_arrive(zz, carry):
        for part in range(2):
            sib_wait(zz, part).wait_recv()
        return carry

    lax.fori_loop(0, n_z, sib_arrive, 0)

    def blocks(ref, s, g):
        one = ref[s, :, g * GW : (g + 1) * GW]
        return jnp.concatenate([one] * GROUP, axis=0) * bdm_ref[...]

    def forward(s, carry):
        keep = jnp.broadcast_to(keep_ref[...][None], (GROUP, 64, 128)) > 0.5
        for g in range(NG):
            sg = s * NG + g
            key_b = blocks(k_ref, s, g)
            value_b = blocks(v_ref, s, g)
            query = qg_ref[s, 0, :, g * GW : (g + 1) * GW]
            gout = qg_ref[s, 1, :, g * GW : (g + 1) * GW]
            scores = dot_nt(key_b, query) * scale + bias_ref[g * 256 : (g + 1) * 256, :]
            scores = jnp.where(keep, scores.reshape(GROUP, 64, 128), NEG)
            top = jnp.max(scores, axis=1)
            expo = jnp.exp(scores - top[:, None, :])
            expo_b = expo.astype(BF)
            pre = dot_nt(value_b, gout).reshape(GROUP, 64, 128)
            st_ref[sg, 0:4, :] = top
            st_ref[sg, 4:8, :] = jnp.sum(expo, axis=1)
            st_ref[sg, 8:12, :] = jnp.sum(expo_b.astype(F32) * pre, axis=1)
            st_ref[sg, 12:16, :] = top
            e_ref[sg] = expo.reshape(256, 128)
            dp_ref[sg] = pre.reshape(256, 128)
            ot_ref[s, g * GW : (g + 1) * GW, :] = dot_tn(value_b, expo_b.reshape(256, 128))
        return carry

    lax.fori_loop(0, 4, forward, 0)

    def b_copy(d):
        c = lax.rem(col + d, n_col)
        return remote(st_ref.at[c], str_ref.at[col], b_send.at[d], b_recv.at[col], at_col(c))

    def b_wait(d):
        c = lax.rem(col + n_col - d, n_col)
        return remote(st_ref.at[c], str_ref.at[c], b_send.at[d], b_recv.at[c], at_col(c))

    def b2_copy(d):
        c = lax.rem(col + d, n_col)
        return remote(res_ref, resr_ref.at[col], b2_send.at[d], b2_recv.at[col], at_col(c))

    def b2_wait(d):
        c = lax.rem(col + n_col - d, n_col)
        return remote(res_ref, resr_ref.at[c], b2_send.at[d], b2_recv.at[c], at_col(c))

    def start_all(make, count):
        def step(d, carry):
            make(d).start()
            return carry

        lax.fori_loop(1, count, step, 0)

    def recv_all(make, count):
        def step(d, carry):
            make(d).wait_recv()
            return carry

        lax.fori_loop(1, count, step, 0)

    def sent_all(make, count):
        def step(d, carry):
            make(d).wait_send()
            return carry

        lax.fori_loop(1, count, step, 0)

    start_all(b_copy, n_col)
    str_ref[col] = st_ref[col]
    recv_all(b_wait, n_col)
    parts = str_ref[...]
    tops = parts[:, 0:4, :]
    top_all = jnp.max(tops, axis=0)
    weight = jnp.exp(tops - top_all[None])
    inv_total = 1.0 / jnp.sum(parts[:, 4:8, :] * weight, axis=0)
    delta = jnp.sum(parts[:, 8:12, :] * weight, axis=0) * inv_total
    res_ref[0:4, :] = top_all
    res_ref[4:8, :] = inv_total
    res_ref[8:12, :] = delta
    res_ref[12:16, :] = delta
    resr_ref[col] = res_ref[...]
    start_all(b2_copy, n_col)
    recv_all(b2_wait, n_col)

    def e_copy(r):
        start = pl.multiple_of(lax.rem(r, 2) * 32, 32)
        return remote(
            dkv_ref.at[r // 2, pl.ds(start, 32), :],
            ekv_ref.at[r // 4, lax.rem(row, 4)],
            e_send.at[r],
            e_recv.at[(r // 4) * 4 + lax.rem(row, 4)],
            at_row((row // 4) * 4 + lax.rem(r, 4)),
        )

    def e_wait(hi, d):
        x = lax.rem(row + 4 - d, 4)
        return remote(
            dkv_ref.at[0, pl.ds(0, 32), :],
            ekv_ref.at[hi, x],
            e_send.at[hi * 4 + x],
            e_recv.at[hi * 4 + x],
            at_row((row // 4) * 4 + x),
        )

    def e_sum(hi):
        for d in range(1, 4):
            e_wait(hi, d).wait_recv()
        r = hi * 4 + lax.rem(row, 4)
        start = pl.multiple_of(lax.rem(r, 2) * 32, 32)
        ekv_ref[hi, lax.rem(row, 4)] = dkv_ref[r // 2, pl.ds(start, 32), :]
        return jnp.sum(ekv_ref[hi], axis=0)

    my_half = pl.multiple_of(core * 64, 64)
    their_half = pl.multiple_of((1 - core) * 64, 64)

    def x_copy(s):
        return remote(
            od_ref.at[s, :, pl.ds(their_half, 64), :],
            ods_ref.at[s],
            x_send.at[s],
            x_recv.at[s],
            sibling,
        )

    lane4 = lax.broadcasted_iota(jnp.int32, (64, GW), 1)

    def diagonal(full):
        picked = full[3 * 64 : 4 * 64]
        for h in (2, 1, 0):
            picked = jnp.where(lane4 < (h + 1) * CH, full[h * 64 : (h + 1) * 64], picked)
        return picked

    def factor_of(sg):
        return jnp.exp(st_ref[sg, 0:4, :] - resr_ref[sg, 0:4, :]) * resr_ref[sg, 4:8, :]

    def bias_copy(g):
        return remote(gbs_ref.at[g], gbr_ref.at[g], f_send.at[g], f_recv.at[g], other_samp)

    def score_grads(g, carry):
        total = jnp.zeros((256, 128), F32)
        for s in range(4):
            sg = s * NG + g
            factor = factor_of(sg)
            down = resr_ref[sg, 8:12, :]
            probs = e_ref[sg].reshape(GROUP, 64, 128) * factor[:, None, :]
            grads = probs * (dp_ref[sg].reshape(GROUP, 64, 128) - down[:, None, :])
            grads = grads.reshape(256, 128)
            total = total + grads
            gr_ref[sg] = grads.astype(BF)
            pr_ref[sg] = probs.reshape(256, 128).astype(BF)
        gbs_ref[g] = total
        bias_copy(g).start()
        return carry

    lax.fori_loop(0, NG, score_grads, 0)

    def query_side(t, carry):
        s = lax.rem(t + rest_row, 4)
        outs, queries = [], []
        for g in range(NG):
            sg = s * NG + g
            part = ot_ref[s, g * GW : (g + 1) * GW, :].reshape(GROUP, CH, 128)
            outs.append((part * factor_of(sg)[:, None, :]).reshape(GW, 128).T)
            queries.append(dot_tn(gr_ref[sg], blocks(k_ref, s, g)) * scale)
        od_ref[s, 0] = jnp.concatenate(outs, axis=1)
        od_ref[s, 1] = jnp.concatenate(queries, axis=1)
        x_copy(s).start()
        return carry

    lax.fori_loop(0, 4, query_side, 0)

    def add_sibling(t, carry):
        s = lax.rem(t + rest_row, 4)
        x_copy(s).wait_recv()
        dqs_ref[s] = od_ref[s, :, pl.ds(my_half, 64), :] + ods_ref[s]
        return carry

    lax.fori_loop(0, 4, add_sibling, 0)

    def own_part(zz, part):
        number = differ(zz, row)
        start = pl.multiple_of(lax.rem(number, 2) * 32 + part * 16, 16)
        return dqs_ref.at[number // 2, :, pl.ds(start, 16), :]

    def rs_copy(way, part, left, src):
        lane_of = part * 2 + (way + 1) // 2
        sem = lane_of * 4 + left - 1
        there = at_col(lax.rem(z + n_z + way, n_z) * 2 + core)
        return remote(src, dqr_ref.at[lane_of, left - 1], d_send.at[sem], d_recv.at[sem], there)

    def rs_slot(way, part, left):
        return dqr_ref.at[part * 2 + (way + 1) // 2, left - 1]

    def rs_first(way, part):
        return 4 if (way == 1) == (part == 0) else 3

    def rs_pass(way, part, left):
        slot = rs_slot(way, part, left)
        rs_copy(way, part, left, slot).wait_recv()
        slot[...] = slot[...] + own_part(lax.rem(z + 2 * n_z + way * (left - 1), n_z), part)[...]
        rs_copy(way, part, left - 1, slot).start()

    for part in range(2):
        for way in (1, -1):
            first = rs_first(way, part)
            target = lax.rem(z + n_z + way * first, n_z)
            rs_copy(way, part, first, own_part(target, part)).start()

    def ring_step(t):
        for part in range(2):
            for way in (1, -1):
                first = rs_first(way, part)

                @pl.when(t < first - 1)
                def _():
                    rs_pass(way, part, first - t)

    def back_project(grad, weight_ref):
        both = dot_nt(jnp.concatenate(split(grad), axis=0), weight_ref[...])
        half = grad.shape[0]
        return both[0:half] + both[half:]

    def backward(t, carry):
        s = lax.rem(t + rest_row, 4)
        keys, values = [], []
        for g in range(NG):
            sg = s * NG + g
            query = qg_ref[s, 0, :, g * GW : (g + 1) * GW]
            gout = qg_ref[s, 1, :, g * GW : (g + 1) * GW]
            keys.append(diagonal(dot_nn(gr_ref[sg], query)) * scale)
            values.append(diagonal(dot_nn(pr_ref[sg], gout)))
        dkv_ref[s] = back_project(jnp.concatenate(keys, axis=1), wk_ref) + back_project(
            jnp.concatenate(values, axis=1), wv_ref
        )
        for half in range(2):
            r = s * 2 + half

            @pl.when(lax.rem(r, 4) != lax.rem(row, 4))
            def _():
                e_copy(r).start()

        ring_step(t)
        return carry

    lax.fori_loop(0, 4, backward, 0)

    ey_copy = remote(
        ey_ref.at[0], ey_ref.at[1], ey_sem.at[0], ey_sem.at[1], at_row(lax.rem(row + 4, n_row))
    )
    ey_ref[0] = e_sum(1 - row // 4)
    ey_copy.start()

    for part in range(2):
        for way in (1, -1):
            rs_copy(way, part, 1, rs_slot(way, part, 1)).wait_recv()
    for part in range(2):
        pm_ref[:, part * 16 : (part + 1) * 16, :] = (
            own_part(z, part)[...] + rs_slot(1, part, 1)[...] + rs_slot(-1, part, 1)[...]
        )
    pm_copy = remote(pm_ref, pmr_ref, pm_sem.at[0], pm_sem.at[1], owner_dev)
    pm_own = pltpu.make_async_copy(pm_ref, pmr_ref, pm_sem.at[2])

    @pl.when(jnp.logical_not(is_self))
    def _():
        pm_copy.start()

    @pl.when(is_self)
    def _():
        pm_own.start()

    def bias_arrive(g, carry):
        bias_copy(g).wait_recv()
        return carry

    lax.fori_loop(0, NG, bias_arrive, 0)
    summed = (gbs_ref[...] + gbr_ref[...]).reshape(H * 64, 128)
    inner = jnp.sum((summed * bias_ref[...]).reshape(H, 64, 128), axis=0) * (1.0 / C)
    bias_ref[...] = summed
    inner_h = inner.astype(BF).astype(F32)
    inner_l = inner - inner_h
    which = lax.broadcasted_iota(jnp.int32, (64, 16, 128), 1)
    inner_ref[...] = jnp.where(
        which == 0, inner_h[:, None, :], jnp.where(which == 1, inner_l[:, None, :], 0.0)
    ).astype(BF)
    weight = wbt.astype(F32) * (total_tokens / samples)
    weight_h, weight_l = split(weight - jnp.mean(weight, axis=1, keepdims=True))
    blank = jnp.zeros((H, C), BF)
    ones = jnp.full((H, C), total_tokens / samples, BF)
    spread_w = jnp.concatenate(
        [
            jnp.concatenate([weight_h, weight_h, weight_l, blank], axis=0),
            jnp.concatenate([blank, blank, blank, ones], axis=0),
        ],
        axis=1,
    )

    def pair_backward(n, acc):
        grads, normeds = [], []
        for u in range(4):
            j = n * 4 + u
            high, low = split(bias_ref[pl.ds(j, H, stride=64), :])
            both = jnp.concatenate([high, low], axis=0)
            normed = nrm_ref[j]
            wide = dot_tn(jnp.concatenate([both, high, inner_ref[j]], axis=0), spread_w)
            raw_ref[pl.ds(j, 128, stride=64), :] = inv_ref[j] * (
                wide[:, 0:C] - normed * wide[:, C:]
            )
            grads.append(both)
            normeds.append(jnp.concatenate(split(normed), axis=1))
        for u in (0, 2):
            acc = acc + dot_nn(
                jnp.concatenate(grads[u : u + 2], axis=1),
                jnp.concatenate(normeds[u : u + 2], axis=0),
            )
        return acc

    acc = lax.fori_loop(0, 16, pair_backward, jnp.zeros((2 * H, 2 * C), F32))

    def weight_copy(d):
        c = lax.rem(col + d, n_col)
        return remote(hs_ref.at[0], hr_ref.at[col], h_send.at[d], h_recv.at[col], at_col(c))

    def weight_wait(d):
        c = lax.rem(col + n_col - d, n_col)
        return remote(hs_ref.at[0], hr_ref.at[c], h_send.at[d], h_recv.at[c], at_col(c))

    hs_ref[0] = (acc[0:H, 0:C] + acc[H:, 0:C]) + (acc[0:H, C:] + acc[H:, C:])
    start_all(weight_copy, n_col)
    hr_ref[col] = hs_ref[0]

    def narrow(n, carry):
        pg_ref[pl.ds(n * 8, 8)] = (
            raw_ref[pl.ds(pl.multiple_of(n * 512, 512), 512), :].reshape(8, 64, C).astype(BF)
        )
        return carry

    lax.fori_loop(0, 16, narrow, 0)

    recv_all(weight_wait, n_col)
    hs_ref[1] = jnp.sum(hr_ref[...], axis=0)

    def weight2_copy(d):
        r = lax.rem(row + d, n_row)
        return remote(hs_ref.at[1], hr2_ref.at[row], h2_send.at[d], h2_recv.at[row], at_row(r))

    def weight2_wait(d):
        r = lax.rem(row + n_row - d, n_row)
        return remote(hs_ref.at[1], hr2_ref.at[r], h2_send.at[d], h2_recv.at[r], at_row(r))

    start_all(weight2_copy, n_row)
    hr2_ref[row] = hs_ref[1]

    total = e_sum(row // 4)
    ey_copy.wait_recv()
    total = total + ey_ref[1]

    @pl.when(jnp.logical_not(is_self))
    def _():
        pm_copy.wait()

    @pl.when(is_self)
    def _():
        pm_own.wait()

    total = total + back_project(pmr_ref[1], wq_ref)
    own_sig = sig_ref[...]
    cot = cot_ref[rest_row, own_rows, :].astype(F32)
    grad_gate = (cot * pmr_ref[0] * own_sig * (1.0 - own_sig)).astype(BF)
    total = total + dot_nt(grad_gate, wg_ref[...])
    own_normed, own_inv = norm(tok_ref[rest_row, own_rows, :].astype(F32) + emb_ref[own_rows, :])
    tg_ref[rest_row, own_rows, :] = norm_back(total, own_normed, own_inv).astype(BF)

    def g_copy(d):
        r = lax.rem(row + d, n_row)
        mine = tg_ref.at[rest_row, own_rows, :]
        return remote(mine, mine, g_send.at[d], g_recv.at[row], at_row(r))

    def g_wait(d):
        r = lax.rem(row + n_row - d, n_row)
        start = pl.multiple_of(lax.rem(r, 2) * 32, 32)
        theirs = tg_ref.at[r // 2, pl.ds(start, 32), :]
        return remote(theirs, theirs, g_send.at[d], g_recv.at[r], at_row(r))

    start_all(g_copy, n_row)
    recv_all(weight2_wait, n_row)
    bw_ref[...] = jnp.sum(hr2_ref[...], axis=0) * (1.0 / samples)

    sent_all(b_copy, n_col)
    sent_all(b2_copy, n_col)
    sent_all(weight_copy, n_col)
    sent_all(weight2_copy, n_row)
    ey_copy.wait_send()
    for part in range(2):
        for way in (1, -1):

            def left_ag(step, carry):
                ag_copy(way, part, step).wait_send()
                return carry

            lax.fori_loop(0, last_step(way, part) + 1, left_ag, 0)

            def left_rs(left, carry):
                rs_copy(way, part, left, rs_slot(way, part, left)).wait_send()
                return carry

            lax.fori_loop(1, rs_first(way, part) + 1, left_rs, 0)

    def left(n, carry):
        for part in range(2):
            sib_copy(n, part).wait_send()

        @pl.when(lax.rem(n, 4) != lax.rem(row, 4))
        def _():
            e_copy(n).wait_send()

        return carry

    lax.fori_loop(0, n_z, left, 0)

    def left_x(s, carry):
        x_copy(s).wait_send()
        bias_copy(s).wait_send()
        return carry

    lax.fori_loop(0, 4, left_x, 0)
    recv_all(g_wait, n_row)
    sent_all(g_copy, n_row)


def body(
    tokens, restype, type_table, key_mask, pair, w_bias, w_query, w_key, w_value, w_gate, cotangent
):
    n_row = lax.axis_size("row")
    n_col = lax.axis_size("col")
    n_z = n_col // 2
    samples = tokens.shape[0] * lax.axis_size("samp")
    total_tokens = tokens.shape[1] * n_col
    vmem = pl.BlockSpec(memory_space=pltpu.VMEM)
    hbm = pl.BlockSpec(memory_space=pl.ANY)
    dma = pltpu.SemaphoreType.DMA
    token_grad, weight_grad, pair_grad = pl.pallas_call(
        functools.partial(kernel, (n_row, n_col, total_tokens, samples)),
        out_shape=(
            pltpu.VMEM((4, 64, D), BF),
            pltpu.VMEM((H, C), F32),
            pltpu.VMEM((128, 64, C), BF),
        ),
        in_specs=[vmem] * 6 + [hbm] * 5,
        out_specs=(vmem, vmem, vmem),
        scratch_shapes=[
            pltpu.VMEM((D, D), BF),
            pltpu.VMEM((D, D), BF),
            pltpu.VMEM((D, D), BF),
            pltpu.VMEM((D, D), BF),
            pltpu.VMEM((128, 64, C), BF),
            pltpu.VMEM((8192, C), F32),
            pltpu.VMEM((64, 128, C), F32),
            pltpu.VMEM((64, 128, C), F32),
            pltpu.VMEM((H * 64, 128), F32),
            pltpu.VMEM((64, D), F32),
            pltpu.VMEM((4, 64, D), BF),
            pltpu.VMEM((4, 64, D), BF),
            pltpu.VMEM((32, D), F32),
            pltpu.VMEM((2, 32, D), BF),
            pltpu.VMEM((4, 2, 128, D), BF),
            pltpu.VMEM((256, GW), BF),
            pltpu.VMEM((64, 128), F32),
            pltpu.VMEM((16, 256, 128), F32),
            pltpu.VMEM((16, 256, 128), F32),
            pltpu.VMEM((4, D, 128), F32),
            pltpu.VMEM((16, 16, 128), F32),
            pltpu.VMEM((16, 16, 128), F32),
            pltpu.VMEM((16, 128), F32),
            pltpu.VMEM((16, 16, 128), F32),
            pltpu.VMEM((NG, 256, 128), F32),
            pltpu.VMEM((NG, 256, 128), F32),
            pltpu.VMEM((16, 256, 128), BF),
            pltpu.VMEM((16, 256, 128), BF),
            pltpu.VMEM((4, 64, D), F32),
            pltpu.VMEM((2, 4, 32, D), F32),
            pltpu.VMEM((2, 32, D), F32),
            pltpu.VMEM((4, 2, 128, D), F32),
            pltpu.VMEM((4, 2, 64, D), F32),
            pltpu.VMEM((4, 2, 64, D), F32),
            pltpu.VMEM((4, 4, 2, 16, D), F32),
            pltpu.VMEM((2, 32, D), F32),
            pltpu.VMEM((2, 32, D), F32),
            pltpu.VMEM((64, 16, 128), BF),
            pltpu.VMEM((n_col, H, C), F32),
            pltpu.VMEM((2, H, C), F32),
            pltpu.VMEM((n_row, H, C), F32),
            dma((4,)),
            dma,
            dma((3,)),
            dma((16,)),
            dma((16,)),
            dma((16,)),
            dma((16,)),
            dma((n_col,)),
            dma((n_col,)),
            dma((n_col,)),
            dma((n_col,)),
            dma((n_row,)),
            dma((n_row,)),
            dma((2,)),
            dma((4,)),
            dma((4,)),
            dma((16,)),
            dma((16,)),
            dma((NG,)),
            dma((NG,)),
            dma((3,)),
            dma((n_row,)),
            dma((n_row,)),
            dma((n_col,)),
            dma((n_col,)),
            dma((n_row,)),
            dma((n_row,)),
        ],
        compiler_params=pltpu.CompilerParams(
            collective_id=0, has_side_effects=True, vmem_limit_bytes=60 * 1024 * 1024
        ),
    )(
        tokens,
        restype.reshape(1, 64),
        type_table,
        key_mask.reshape(1, 64),
        w_bias.T,
        cotangent,
        w_query,
        w_key,
        w_value,
        w_gate,
        pair,
    )
    return (token_grad, pair_grad, weight_grad.T)


def solution(mesh):
    placed = (
        P("samp", "col", None),
        P("col"),
        P(),
        P("col"),
        P("row", "col", None),
        P(),
        P(),
        P(),
        P(),
        P(),
        P("samp", "col", None),
    )
    return jax.shard_map(
        body,
        mesh=mesh,
        in_specs=placed,
        out_specs=(P("samp", "col", None), P("row", "col", None), P()),
        check_vma=False,
    )
```

time: 164 us -> 116 us (0.71)
  Pallas kernels: 154 us -> 113 us
  local copies, waits for them, and re-layouts: 8.18 us -> 2.66 us
    pallas_call x1, Pallas kernels: 154 us -> 113 us  [body(): pl.pallas_call(functools.partial(kernel, (n_row, n_col, total_tokens, sam...]
    unnamed x5 -> x3, local copies, waits for them, and re-layouts: 5.46 us -> 2.66 us
    reshape x2 -> x0, local copies, waits for them, and re-layouts: 2.72 us -> none  [the longest x1 1.36 us: body(): restype.reshape(64, 1)]
where the time goes in v2:
time: 116 us
  Pallas kernels  113 us (97%)
  local copies, waits for them, and re-layouts  2.66 us (2%)
    pallas_call x1, Pallas kernels, body(): pl.pallas_call(functools.partial(kernel, (n_row, n_col, total_tokens, sam...  113 us
    unnamed x3, local copies, waits for them, and re-layouts  2.66 us

profile of v2, /device:TPU:8, one launch (start us, length us, event | category | flops | bytes accessed | tf_op | source)
XLA Modules:
  0.0 115.8 jit_solution(13110626579309212666)
XLA Ops:
  0.6 112.5 %shard_map.130 = (bf16[4,64,768]{2,1,0:T(8,128)(2,1)S(1)}, f32[16,128]{1,0:T(8,128)S(1)}, bf16[128,64,128]{2,1,0:T(8,128)(2,1)S(1)}) custom-call(bf16[4,64,768]{2,1,0:T(8,128)(2,1)} %tok_ref.1, s32[1,64]{1,0:T(1,128)} %bitcast.6, bf16[32,768]{1,0:T(8,128)(2,1)} %table_ref.1, s32[1,64]{1,0:T(1,128)} %bitcast.7, bf16[16,128]{1,0:T(8,128)(2,1)} %bitcast.5, ...), custom_call_target="tpu_custom_call" | custom-call | tf_op jit(solution)/shard_map/pallas_call | solution.py:815
  113.2 0.7 copy.17
  113.9 0.6 copy.19
  114.5 1.3 %copy.18 = bf16[128,64,128]{2,1,0:T(8,128)(2,1)} copy(bf16[128,64,128]{2,1,0:T(8,128)(2,1)S(1)} %get-tuple-element.10) | data formatting | bytes 4194304

commit v3 on v2

--- a/solution.py
+++ b/solution.py
@@ -101,9 +101,13 @@
     dkv_ref,
     ekv_ref,
     ey_ref,
-    od_ref,
-    ods_ref,
+    oa_ref,
+    oas_ref,
+    oa_ref2,
+    or_ref,
+    dq_ref,
     dqs_ref,
+    dq_ref2,
     dqr_ref,
     pm_ref,
     pmr_ref,
@@ -125,8 +129,12 @@
     e_send,
     e_recv,
     ey_sem,
+    y_send,
+    y_recv,
     x_send,
     x_recv,
+    o_send,
+    o_recv,
     d_send,
     d_recv,
     f_send,
@@ -215,14 +223,59 @@
     own_rows = pl.ds(own_tok, 32)
     own_normed, own_inv = norm(tok_ref[rest_row, own_rows, :].astype(F32) + emb_ref[own_rows, :])
     own_act = own_normed.astype(BF)
+    def region(number, part):
+        start = pl.multiple_of(core * 64 + lax.rem(number, 2) * 32, 32)
+        return qg_ref.at[number // 2, part, pl.ds(start, 32), :]
+
+    def to_query(part):
+        mine = qgs_ref.at[part]
+        return remote(mine, region(row, part), t_sem.at[part], t_sem.at[2 + part], query_dev)
+
+    def to_self(part):
+        return pltpu.make_async_copy(
+            qgs_ref.at[part], region(slice_here, part), t_sem.at[4 + part]
+        )
+
+    def swap_start(part):
+        @pl.when(jnp.logical_not(is_self))
+        def _():
+            to_query(part).start()
+
+        @pl.when(is_self)
+        def _():
+            to_self(part).start()
+
+    def swap_wait(part):
+        @pl.when(jnp.logical_not(is_self))
+        def _():
+            theirs = region(slice_here, part)
+            remote(
+                qgs_ref.at[part], theirs, t_sem.at[part], t_sem.at[2 + part], owner_dev
+            ).wait_recv()
+
+        @pl.when(is_self)
+        def _():
+            to_self(part).wait()
+
     weights[0].wait()
     qgs_ref[0] = dot_nn(own_act, wq_ref[...]).astype(BF)
+
+    @pl.when(is_self)
+    def _():
+        pl.semaphore_wait(barrier, n_col + n_row - 1)
+
+    @pl.when(jnp.logical_not(is_self))
+    def _():
+        pl.semaphore_wait(barrier, n_col + n_row + 1)
+
+    swap_start(0)
     weights[1].wait()
     gate = dot_nn(own_act, wg_ref[...]).astype(BF).astype(F32)
     sig = jax.nn.sigmoid(gate)
     sig_ref[...] = sig
     own_cot = cot_ref[rest_row, own_rows, :].astype(F32)
     qgs_ref[1] = (own_cot * sig).astype(BF)
+    swap_start(1)
 
     weights[2].wait()
     weights[3].wait()
@@ -242,7 +295,6 @@
     first_row = lax.broadcasted_iota(jnp.int32, (16, 64), 0) == 0
     kept = jnp.where(jnp.logical_and(mask_ref[...] == 1, first_row), 1.0, 0.0)
     keep_ref[...] = dot_tn(kept.astype(BF), jnp.ones((16, 128), BF))
-
     pair_copy.wait()
 
     def widen(n, carry):
@@ -252,39 +304,6 @@
         return carry
 
     lax.fori_loop(0, 16, widen, 0)
-    @pl.when(is_self)
-    def _():
-        pl.semaphore_wait(barrier, n_col + n_row - 1)
-
-    @pl.when(jnp.logical_not(is_self))
-    def _():
-        pl.semaphore_wait(barrier, n_col + n_row + 1)
-
-    def region(number):
-        start = pl.multiple_of(core * 64 + lax.rem(number, 2) * 32, 32)
-        return qg_ref.at[number // 2, :, pl.ds(start, 32), :]
-
-    to_swapped = remote(qgs_ref, region(row), t_sem.at[0], t_sem.at[1], query_dev)
-    from_swapped = remote(qgs_ref, region(slice_here), t_sem.at[0], t_sem.at[1], owner_dev)
-    keep_own = pltpu.make_async_copy(qgs_ref, region(slice_here), t_sem.at[2])
-
-    @pl.when(jnp.logical_not(is_self))
-    def _():
-        to_swapped.start()
-
-    @pl.when(is_self)
-    def _():
-        keep_own.start()
-
-    @pl.when(jnp.logical_not(is_self))
-    def _():
-        to_swapped.wait_send()
-        from_swapped.wait_recv()
-
-    @pl.when(is_self)
-    def _():
-        keep_own.wait()
-
     def part_of(zz, kk, part):
         number = differ(zz, row)
         start = pl.multiple_of(kk * 64 + lax.rem(number, 2) * 32, 32)
@@ -315,11 +334,6 @@
 
     def last_step(way, part):
         return 3 if (way == 1) == (part == 0) else 2
-
-    for part in range(2):
-        for way in (1, -1):
-            ag_copy(way, part, 0).start()
-        sib_copy(z, part).start()
 
     wbt = wbt_ref[...]
     wbt_wide = jnp.concatenate([wbt, wbt], axis=1)
@@ -344,10 +358,15 @@
             )
         return carry
 
+    lax.fori_loop(0, 8, pair_forward, 0)
+    for part in range(2):
+        swap_wait(part)
+        for way in (1, -1):
+            ag_copy(way, part, 0).start()
+        sib_copy(z, part).start()
+
     def gather_step(step, carry):
         for part in range(2):
-            for n in range(2):
-                pair_forward(step * 4 + part * 2 + n, 0)
             for way in (1, -1):
 
                 @pl.when(step <= last_step(way, part))
@@ -364,7 +383,12 @@
 
         return carry
 
-    lax.fori_loop(0, 4, gather_step, 0)
+    def gather_and_pair(step, carry):
+        for n in range(2):
+            pair_forward(8 + step * 2 + n, 0)
+        return gather_step(step, carry)
+
+    lax.fori_loop(0, 4, gather_and_pair, 0)
 
     def sib_arrive(zz, carry):
         for part in range(2):
@@ -376,6 +400,13 @@
     def blocks(ref, s, g):
         one = ref[s, :, g * GW : (g + 1) * GW]
         return jnp.concatenate([one] * GROUP, axis=0) * bdm_ref[...]
+
+    def b_copy(c):
+        return remote(st_ref.at[c], str_ref.at[col], b_send.at[c], b_recv.at[col], at_col(c))
+
+    def b_wait(d):
+        c = lax.rem(col + n_col - d, n_col)
+        return remote(st_ref.at[c], str_ref.at[c], b_send.at[c], b_recv.at[c], at_col(c))
 
     def forward(s, carry):
         keep = jnp.broadcast_to(keep_ref[...][None], (GROUP, 64, 128)) > 0.5
@@ -394,21 +425,17 @@
             st_ref[sg, 0:4, :] = top
             st_ref[sg, 4:8, :] = jnp.sum(expo, axis=1)
             st_ref[sg, 8:12, :] = jnp.sum(expo_b.astype(F32) * pre, axis=1)
-            st_ref[sg, 12:16, :] = top
             e_ref[sg] = expo.reshape(256, 128)
             dp_ref[sg] = pre.reshape(256, 128)
+
+            @pl.when(sg != col)
+            def _():
+                b_copy(sg).start()
+
             ot_ref[s, g * GW : (g + 1) * GW, :] = dot_tn(value_b, expo_b.reshape(256, 128))
         return carry
 
     lax.fori_loop(0, 4, forward, 0)
-
-    def b_copy(d):
-        c = lax.rem(col + d, n_col)
-        return remote(st_ref.at[c], str_ref.at[col], b_send.at[d], b_recv.at[col], at_col(c))
-
-    def b_wait(d):
-        c = lax.rem(col + n_col - d, n_col)
-        return remote(st_ref.at[c], str_ref.at[c], b_send.at[d], b_recv.at[c], at_col(c))
 
     def b2_copy(d):
         c = lax.rem(col + d, n_col)
@@ -439,7 +466,6 @@
 
         lax.fori_loop(1, count, step, 0)
 
-    start_all(b_copy, n_col)
     str_ref[col] = st_ref[col]
     recv_all(b_wait, n_col)
     parts = str_ref[...]
@@ -451,7 +477,6 @@
     res_ref[0:4, :] = top_all
     res_ref[4:8, :] = inv_total
     res_ref[8:12, :] = delta
-    res_ref[12:16, :] = delta
     resr_ref[col] = res_ref[...]
     start_all(b2_copy, n_col)
     recv_all(b2_wait, n_col)
@@ -487,14 +512,109 @@
     my_half = pl.multiple_of(core * 64, 64)
     their_half = pl.multiple_of((1 - core) * 64, 64)
 
-    def x_copy(s):
-        return remote(
-            od_ref.at[s, :, pl.ds(their_half, 64), :],
-            ods_ref.at[s],
-            x_send.at[s],
-            x_recv.at[s],
-            sibling,
-        )
+    def core_copy(src, dst, send, recv):
+        def make(s):
+            half = src.at[s, pl.ds(their_half, 64), :]
+            return remote(half, dst.at[s], send.at[s], recv.at[s], sibling)
+
+        return make
+
+    y_copy = core_copy(oa_ref, oas_ref, y_send, y_recv)
+    x_copy = core_copy(dq_ref, dqs_ref, x_send, x_recv)
+
+    def first_left(way, part):
+        return 4 if (way == 1) == (part == 0) else 3
+
+    def ring(own, slots, send, recv):
+        def own_part(zz, part):
+            number = differ(zz, row)
+            start = pl.multiple_of(lax.rem(number, 2) * 32 + part * 16, 16)
+            return own.at[number // 2, pl.ds(start, 16), :]
+
+        def slot(way, part, left):
+            return slots.at[part * 2 + (way + 1) // 2, left - 1]
+
+        def copy(way, part, left, src):
+            sem = (part * 2 + (way + 1) // 2) * 4 + left - 1
+            there = at_col(lax.rem(z + n_z + way, n_z) * 2 + core)
+            return remote(src, slot(way, part, left), send.at[sem], recv.at[sem], there)
+
+        def begin():
+            for part in range(2):
+                for way in (1, -1):
+                    left = first_left(way, part)
+                    target = lax.rem(z + n_z + way * left, n_z)
+                    copy(way, part, left, own_part(target, part)).start()
+
+        def step(t):
+            for part in range(2):
+                for way in (1, -1):
+                    left = first_left(way, part) - t
+
+                    @pl.when(left > 1)
+                    def _():
+                        here = slot(way, part, left)
+                        copy(way, part, left, here).wait_recv()
+                        target = lax.rem(z + 2 * n_z + way * (left - 1), n_z)
+                        here[...] = here[...] + own_part(target, part)[...]
+                        copy(way, part, left - 1, here).start()
+
+        def finish(dst):
+            for part in range(2):
+                for way in (1, -1):
+                    copy(way, part, 1, slot(way, part, 1)).wait_recv()
+            for part in range(2):
+                dst[part * 16 : (part + 1) * 16, :] = (
+                    own_part(z, part)[...] + slot(1, part, 1)[...] + slot(-1, part, 1)[...]
+                )
+
+        def drain():
+            for part in range(2):
+                for way in (1, -1):
+
+                    def sent(left, carry):
+                        copy(way, part, left, slot(way, part, left)).wait_send()
+                        return carry
+
+                    lax.fori_loop(1, first_left(way, part) + 1, sent, 0)
+
+        return begin, step, finish, drain
+
+    o_begin, o_step, o_finish, o_drain = ring(oa_ref2, or_ref, o_send, o_recv)
+    d_begin, d_step, d_finish, d_drain = ring(dq_ref2, dqr_ref, d_send, d_recv)
+
+    def add_cores(copy, whole, other, out):
+        def step(t, carry):
+            s = lax.rem(t + rest_row, 4)
+            copy(s).wait_recv()
+            out[s] = whole[s, pl.ds(my_half, 64), :] + other[s]
+            return carry
+
+        lax.fori_loop(0, 4, step, 0)
+
+    def hand_over(n):
+        return remote(pm_ref.at[n], pmr_ref.at[n], pm_sem.at[n], pm_sem.at[2 + n], owner_dev)
+
+    def hand_own(n):
+        return pltpu.make_async_copy(pm_ref.at[n], pmr_ref.at[n], pm_sem.at[4 + n])
+
+    def hand_start(n):
+        @pl.when(jnp.logical_not(is_self))
+        def _():
+            hand_over(n).start()
+
+        @pl.when(is_self)
+        def _():
+            hand_own(n).start()
+
+    def hand_wait(n):
+        @pl.when(jnp.logical_not(is_self))
+        def _():
+            hand_over(n).wait()
+
+        @pl.when(is_self)
+        def _():
+            hand_own(n).wait()
 
     lane4 = lax.broadcasted_iota(jnp.int32, (64, GW), 1)
 
@@ -506,6 +626,18 @@
 
     def factor_of(sg):
         return jnp.exp(st_ref[sg, 0:4, :] - resr_ref[sg, 0:4, :]) * resr_ref[sg, 4:8, :]
+
+    def attended(t, carry):
+        s = lax.rem(t + rest_row, 4)
+        outs = []
+        for g in range(NG):
+            part = ot_ref[s, g * GW : (g + 1) * GW, :].reshape(GROUP, CH, 128)
+            outs.append((part * factor_of(s * NG + g)[:, None, :]).reshape(GW, 128).T)
+        oa_ref[s] = jnp.concatenate(outs, axis=1)
+        y_copy(s).start()
+        return carry
+
+    lax.fori_loop(0, 4, attended, 0)
 
     def bias_copy(g):
         return remote(gbs_ref.at[g], gbr_ref.at[g], f_send.at[g], f_recv.at[g], other_samp)
@@ -528,66 +660,22 @@
 
     lax.fori_loop(0, NG, score_grads, 0)
 
+    add_cores(y_copy, oa_ref, oas_ref, oa_ref2)
+    o_begin()
+
     def query_side(t, carry):
         s = lax.rem(t + rest_row, 4)
-        outs, queries = [], []
+        queries = []
         for g in range(NG):
-            sg = s * NG + g
-            part = ot_ref[s, g * GW : (g + 1) * GW, :].reshape(GROUP, CH, 128)
-            outs.append((part * factor_of(sg)[:, None, :]).reshape(GW, 128).T)
-            queries.append(dot_tn(gr_ref[sg], blocks(k_ref, s, g)) * scale)
-        od_ref[s, 0] = jnp.concatenate(outs, axis=1)
-        od_ref[s, 1] = jnp.concatenate(queries, axis=1)
+            queries.append(dot_tn(gr_ref[s * NG + g], blocks(k_ref, s, g)) * scale)
+        dq_ref[s] = jnp.concatenate(queries, axis=1)
         x_copy(s).start()
         return carry
 
     lax.fori_loop(0, 4, query_side, 0)
-
-    def add_sibling(t, carry):
-        s = lax.rem(t + rest_row, 4)
-        x_copy(s).wait_recv()
-        dqs_ref[s] = od_ref[s, :, pl.ds(my_half, 64), :] + ods_ref[s]
-        return carry
-
-    lax.fori_loop(0, 4, add_sibling, 0)
-
-    def own_part(zz, part):
-        number = differ(zz, row)
-        start = pl.multiple_of(lax.rem(number, 2) * 32 + part * 16, 16)
-        return dqs_ref.at[number // 2, :, pl.ds(start, 16), :]
-
-    def rs_copy(way, part, left, src):
-        lane_of = part * 2 + (way + 1) // 2
-        sem = lane_of * 4 + left - 1
-        there = at_col(lax.rem(z + n_z + way, n_z) * 2 + core)
-        return remote(src, dqr_ref.at[lane_of, left - 1], d_send.at[sem], d_recv.at[sem], there)
-
-    def rs_slot(way, part, left):
-        return dqr_ref.at[part * 2 + (way + 1) // 2, left - 1]
-
-    def rs_first(way, part):
-        return 4 if (way == 1) == (part == 0) else 3
-
-    def rs_pass(way, part, left):
-        slot = rs_slot(way, part, left)
-        rs_copy(way, part, left, slot).wait_recv()
-        slot[...] = slot[...] + own_part(lax.rem(z + 2 * n_z + way * (left - 1), n_z), part)[...]
-        rs_copy(way, part, left - 1, slot).start()
-
-    for part in range(2):
-        for way in (1, -1):
-            first = rs_first(way, part)
-            target = lax.rem(z + n_z + way * first, n_z)
-            rs_copy(way, part, first, own_part(target, part)).start()
-
-    def ring_step(t):
-        for part in range(2):
-            for way in (1, -1):
-                first = rs_first(way, part)
-
-                @pl.when(t < first - 1)
-                def _():
-                    rs_pass(way, part, first - t)
+    add_cores(x_copy, dq_ref, dqs_ref, dq_ref2)
+    d_begin()
+    o_step(0)
 
     def back_project(grad, weight_ref):
         both = dot_nt(jnp.concatenate(split(grad), axis=0), weight_ref[...])
@@ -613,34 +701,15 @@
             def _():
                 e_copy(r).start()
 
-        ring_step(t)
-        return carry
-
-    lax.fori_loop(0, 4, backward, 0)
-
-    ey_copy = remote(
-        ey_ref.at[0], ey_ref.at[1], ey_sem.at[0], ey_sem.at[1], at_row(lax.rem(row + 4, n_row))
-    )
-    ey_ref[0] = e_sum(1 - row // 4)
-    ey_copy.start()
-
-    for part in range(2):
-        for way in (1, -1):
-            rs_copy(way, part, 1, rs_slot(way, part, 1)).wait_recv()
-    for part in range(2):
-        pm_ref[:, part * 16 : (part + 1) * 16, :] = (
-            own_part(z, part)[...] + rs_slot(1, part, 1)[...] + rs_slot(-1, part, 1)[...]
-        )
-    pm_copy = remote(pm_ref, pmr_ref, pm_sem.at[0], pm_sem.at[1], owner_dev)
-    pm_own = pltpu.make_async_copy(pm_ref, pmr_ref, pm_sem.at[2])
-
-    @pl.when(jnp.logical_not(is_self))
-    def _():
-        pm_copy.start()
-
-    @pl.when(is_self)
-    def _():
-        pm_own.start()
+        return carry
+
+    def backward_and_pass(n, carry):
+        lax.fori_loop(n * 2, n * 2 + 2, backward, 0)
+        o_step(n + 1)
+        d_step(n)
+        return carry
+
+    lax.fori_loop(0, 2, backward_and_pass, 0)
 
     def bias_arrive(g, carry):
         bias_copy(g).wait_recv()
@@ -688,7 +757,17 @@
             )
         return acc
 
-    acc = lax.fori_loop(0, 16, pair_backward, jnp.zeros((2 * H, 2 * C), F32))
+    acc = lax.fori_loop(0, 8, pair_backward, jnp.zeros((2 * H, 2 * C), F32))
+    d_step(2)
+    o_finish(pm_ref.at[0])
+    hand_start(0)
+
+    ey_copy = remote(
+        ey_ref.at[0], ey_ref.at[1], ey_sem.at[0], ey_sem.at[1], at_row(lax.rem(row + 4, n_row))
+    )
+    ey_ref[0] = e_sum(1 - row // 4)
+    ey_copy.start()
+    acc = lax.fori_loop(8, 16, pair_backward, acc)
 
     def weight_copy(d):
         c = lax.rem(col + d, n_col)
@@ -701,6 +780,8 @@
     hs_ref[0] = (acc[0:H, 0:C] + acc[H:, 0:C]) + (acc[0:H, C:] + acc[H:, C:])
     start_all(weight_copy, n_col)
     hr_ref[col] = hs_ref[0]
+    d_finish(pm_ref.at[1])
+    hand_start(1)
 
     def narrow(n, carry):
         pg_ref[pl.ds(n * 8, 8)] = (
@@ -728,14 +809,8 @@
     ey_copy.wait_recv()
     total = total + ey_ref[1]
 
-    @pl.when(jnp.logical_not(is_self))
-    def _():
-        pm_copy.wait()
-
-    @pl.when(is_self)
-    def _():
-        pm_own.wait()
-
+    hand_wait(0)
+    hand_wait(1)
     total = total + back_project(pmr_ref[1], wq_ref)
     own_sig = sig_ref[...]
     cot = cot_ref[rest_row, own_rows, :].astype(F32)
@@ -759,11 +834,17 @@
     recv_all(weight2_wait, n_row)
     bw_ref[...] = jnp.sum(hr2_ref[...], axis=0) * (1.0 / samples)
 
-    sent_all(b_copy, n_col)
+    @pl.when(jnp.logical_not(is_self))
+    def _():
+        for part in range(2):
+            to_query(part).wait_send()
+
     sent_all(b2_copy, n_col)
     sent_all(weight_copy, n_col)
     sent_all(weight2_copy, n_row)
     ey_copy.wait_send()
+    o_drain()
+    d_drain()
     for part in range(2):
         for way in (1, -1):
 
@@ -773,12 +854,6 @@
 
             lax.fori_loop(0, last_step(way, part) + 1, left_ag, 0)
 
-            def left_rs(left, carry):
-                rs_copy(way, part, left, rs_slot(way, part, left)).wait_send()
-                return carry
-
-            lax.fori_loop(1, rs_first(way, part) + 1, left_rs, 0)
-
     def left(n, carry):
         for part in range(2):
             sib_copy(n, part).wait_send()
@@ -791,8 +866,18 @@
 
     lax.fori_loop(0, n_z, left, 0)
 
+    def left_b(c, carry):
+        @pl.when(c != col)
+        def _():
+            b_copy(c).wait_send()
+
+        return carry
+
+    lax.fori_loop(0, n_col, left_b, 0)
+
     def left_x(s, carry):
         x_copy(s).wait_send()
+        y_copy(s).wait_send()
         bias_copy(s).wait_send()
         return carry
 
@@ -842,10 +927,10 @@
             pltpu.VMEM((16, 256, 128), F32),
             pltpu.VMEM((16, 256, 128), F32),
             pltpu.VMEM((4, D, 128), F32),
-            pltpu.VMEM((16, 16, 128), F32),
-            pltpu.VMEM((16, 16, 128), F32),
-            pltpu.VMEM((16, 128), F32),
-            pltpu.VMEM((16, 16, 128), F32),
+            pltpu.VMEM((16, 12, 128), F32),
+            pltpu.VMEM((16, 12, 128), F32),
+            pltpu.VMEM((12, 128), F32),
+            pltpu.VMEM((16, 12, 128), F32),
             pltpu.VMEM((NG, 256, 128), F32),
             pltpu.VMEM((NG, 256, 128), F32),
             pltpu.VMEM((16, 256, 128), BF),
@@ -853,10 +938,14 @@
             pltpu.VMEM((4, 64, D), F32),
             pltpu.VMEM((2, 4, 32, D), F32),
             pltpu.VMEM((2, 32, D), F32),
-            pltpu.VMEM((4, 2, 128, D), F32),
-            pltpu.VMEM((4, 2, 64, D), F32),
-            pltpu.VMEM((4, 2, 64, D), F32),
-            pltpu.VMEM((4, 4, 2, 16, D), F32),
+            pltpu.VMEM((4, 128, D), F32),
+            pltpu.VMEM((4, 64, D), F32),
+            pltpu.VMEM((4, 64, D), F32),
+            pltpu.VMEM((4, 4, 16, D), F32),
+            pltpu.VMEM((4, 128, D), F32),
+            pltpu.VMEM((4, 64, D), F32),
+            pltpu.VMEM((4, 64, D), F32),
+            pltpu.VMEM((4, 4, 16, D), F32),
             pltpu.VMEM((2, 32, D), F32),
             pltpu.VMEM((2, 32, D), F32),
             pltpu.VMEM((64, 16, 128), BF),
@@ -865,7 +954,7 @@
             pltpu.VMEM((n_row, H, C), F32),
             dma((4,)),
             dma,
-            dma((3,)),
+            dma((6,)),
             dma((16,)),
             dma((16,)),
             dma((16,)),
@@ -879,11 +968,15 @@
             dma((2,)),
             dma((4,)),
             dma((4,)),
+            dma((4,)),
+            dma((4,)),
+            dma((16,)),
+            dma((16,)),
             dma((16,)),
             dma((16,)),
             dma((NG,)),
             dma((NG,)),
-            dma((3,)),
+            dma((6,)),
             dma((n_row,)),
             dma((n_row,)),
             dma((n_col,)),

time: 116 us -> 109 us (0.940)
  Pallas kernels: 113 us -> 105 us
    pallas_call x1, Pallas kernels: 113 us -> 105 us  [body(): pl.pallas_call(functools.partial(kernel, (n_row, n_col, total_tokens, sam...]
where the time goes in v3:
time: 109 us
  Pallas kernels  105 us (96%)
  local copies, waits for them, and re-layouts  2.66 us (2%)
    pallas_call x1, Pallas kernels, body(): pl.pallas_call(functools.partial(kernel, (n_row, n_col, total_tokens, sam...  105 us
    unnamed x3, local copies, waits for them, and re-layouts  2.66 us

profile of v3, /device:TPU:8, one launch (start us, length us, event | category | flops | bytes accessed | tf_op | source)
XLA Modules:
  0.0 108.7 jit_solution(17591118137524614261)
XLA Ops:
  0.6 105.4 %shard_map.130 = (bf16[4,64,768]{2,1,0:T(8,128)(2,1)S(1)}, f32[16,128]{1,0:T(8,128)S(1)}, bf16[128,64,128]{2,1,0:T(8,128)(2,1)S(1)}) custom-call(bf16[4,64,768]{2,1,0:T(8,128)(2,1)} %tok_ref.1, s32[1,64]{1,0:T(1,128)} %bitcast.6, bf16[32,768]{1,0:T(8,128)(2,1)} %table_ref.1, s32[1,64]{1,0:T(1,128)} %bitcast.7, bf16[16,128]{1,0:T(8,128)(2,1)} %bitcast.5, ...), custom_call_target="tpu_custom_call" | custom-call | tf_op jit(solution)/shard_map/pallas_call | solution.py:900
  106.0 0.7 copy.17
  106.7 0.6 copy.19
  107.3 1.3 %copy.18 = bf16[128,64,128]{2,1,0:T(8,128)(2,1)} copy(bf16[128,64,128]{2,1,0:T(8,128)(2,1)S(1)} %get-tuple-element.10) | data formatting | bytes 4194304

commit v4 on v3

--- a/solution.py
+++ b/solution.py
@@ -185,6 +185,28 @@
             device_id_type=MESH,
         )
 
+    barrier = pltpu.get_barrier_semaphore()
+
+    def greet(device):
+        pl.semaphore_signal(barrier, inc=1, device_id=device, device_id_type=MESH)
+
+    def greet_col(d, carry):
+        greet(at_col(lax.rem(col + d, n_col)))
+        return carry
+
+    def greet_row(d, carry):
+        greet(at_row(lax.rem(row + d, n_row)))
+        return carry
+
+    lax.fori_loop(1, n_col, greet_col, 0)
+    lax.fori_loop(1, n_row, greet_row, 0)
+    greet(other_samp)
+
+    @pl.when(jnp.logical_not(is_self))
+    def _():
+        greet(query_dev)
+        greet(owner_dev)
+
     weights = [
         pltpu.make_async_copy(src, dst, w_sem.at[n])
         for n, (src, dst) in enumerate(
@@ -195,28 +217,6 @@
         copy.start()
     pair_copy = pltpu.make_async_copy(pair_hbm, pair_ref, pair_sem)
     pair_copy.start()
-
-    barrier = pltpu.get_barrier_semaphore()
-
-    def greet(device):
-        pl.semaphore_signal(barrier, inc=1, device_id=device, device_id_type=MESH)
-
-    def greet_col(d, carry):
-        greet(at_col(lax.rem(col + d, n_col)))
-        return carry
-
-    def greet_row(d, carry):
-        greet(at_row(lax.rem(row + d, n_row)))
-        return carry
-
-    lax.fori_loop(1, n_col, greet_col, 0)
-    lax.fori_loop(1, n_row, greet_row, 0)
-    greet(other_samp)
-
-    @pl.when(jnp.logical_not(is_self))
-    def _():
-        greet(query_dev)
-        greet(owner_dev)
 
     onehot = jnp.where(rest_ref[...] == lax.broadcasted_iota(jnp.int32, (NTYPE, 64), 0), 1.0, 0.0)
     emb_ref[...] = dot_tn(onehot.astype(BF), table_ref[...])
@@ -432,7 +432,12 @@
             def _():
                 b_copy(sg).start()
 
-            ot_ref[s, g * GW : (g + 1) * GW, :] = dot_tn(value_b, expo_b.reshape(256, 128))
+        return carry
+
+    def partial_out(s, carry):
+        for g in range(NG):
+            expo_b = e_ref[s * NG + g].astype(BF)
+            ot_ref[s, g * GW : (g + 1) * GW, :] = dot_tn(blocks(v_ref, s, g), expo_b)
         return carry
 
     lax.fori_loop(0, 4, forward, 0)
@@ -467,6 +472,7 @@
         lax.fori_loop(1, count, step, 0)
 
     str_ref[col] = st_ref[col]
+    lax.fori_loop(0, 4, partial_out, 0)
     recv_all(b_wait, n_col)
     parts = str_ref[...]
     tops = parts[:, 0:4, :]
@@ -809,14 +815,14 @@
     ey_copy.wait_recv()
     total = total + ey_ref[1]
 
+    own_normed, own_inv = norm(tok_ref[rest_row, own_rows, :].astype(F32) + emb_ref[own_rows, :])
+    own_sig = sig_ref[...]
+    cot = cot_ref[rest_row, own_rows, :].astype(F32)
     hand_wait(0)
+    grad_gate = (cot * pmr_ref[0] * own_sig * (1.0 - own_sig)).astype(BF)
+    total = total + dot_nt(grad_gate, wg_ref[...])
     hand_wait(1)
     total = total + back_project(pmr_ref[1], wq_ref)
-    own_sig = sig_ref[...]
-    cot = cot_ref[rest_row, own_rows, :].astype(F32)
-    grad_gate = (cot * pmr_ref[0] * own_sig * (1.0 - own_sig)).astype(BF)
-    total = total + dot_nt(grad_gate, wg_ref[...])
-    own_normed, own_inv = norm(tok_ref[rest_row, own_rows, :].astype(F32) + emb_ref[own_rows, :])
     tg_ref[rest_row, own_rows, :] = norm_back(total, own_normed, own_inv).astype(BF)
 
     def g_copy(d):

time: 109 us -> 108 us (level)
    pallas_call x1, Pallas kernels: 105 us -> 104 us  [body(): pl.pallas_call(functools.partial(kernel, (n_row, n_col, total_tokens, sam...]
where the time goes in v4:
time: 108 us; the launch traced here: 107 us
  Pallas kernels  104 us (96%)
  local copies, waits for them, and re-layouts  2.66 us (2%)
    pallas_call x1, Pallas kernels, body(): pl.pallas_call(functools.partial(kernel, (n_row, n_col, total_tokens, sam...  104 us
    unnamed x3, local copies, waits for them, and re-layouts  2.66 us

profile of v4, /device:TPU:8, one launch (start us, length us, event | category | flops | bytes accessed | tf_op | source)
XLA Modules:
  0.0 107.4 jit_solution(17429741676057864963)
XLA Ops:
  0.6 104.1 %shard_map.130 = (bf16[4,64,768]{2,1,0:T(8,128)(2,1)S(1)}, f32[16,128]{1,0:T(8,128)S(1)}, bf16[128,64,128]{2,1,0:T(8,128)(2,1)S(1)}) custom-call(bf16[4,64,768]{2,1,0:T(8,128)(2,1)} %tok_ref.1, s32[1,64]{1,0:T(1,128)} %bitcast.6, bf16[32,768]{1,0:T(8,128)(2,1)} %table_ref.1, s32[1,64]{1,0:T(1,128)} %bitcast.7, bf16[16,128]{1,0:T(8,128)(2,1)} %bitcast.5, ...), custom_call_target="tpu_custom_call" | custom-call | tf_op jit(solution)/shard_map/pallas_call | solution.py:906
  104.8 0.7 copy.17
  105.5 0.6 copy.19
  106.1 1.3 %copy.18 = bf16[128,64,128]{2,1,0:T(8,128)(2,1)} copy(bf16[128,64,128]{2,1,0:T(8,128)(2,1)S(1)} %get-tuple-element.10) | data formatting | bytes 4194304
